TPU v7x, 32 devices: a whole 2x2x4 slice. The times are simulated.
32 devices in a mesh: batch: 8 (over z, y), head: 4 (over x, core).
Axes of the slice: x: 2, y: 2, z: 4, core: 2. Of those that a mesh axis runs over, the one named last changes fastest.
Arguments:
- residual: float32 [8192, 768], P('batch'), may hold values from -6 to 6
- cotangent: float32 [8192, 768], P('batch'), may hold values from -6 to 6
- lengths: int32 [8], P('batch'), may hold values from 1 to 1024, as said below
- gains: float32 [2, 768], replicated, may hold values from 0.5 to 1.5
- heads_weight: float32 [768, 3, 768], P(None, None, 'head'), may hold values from -0.21875 to 0.21875
- merge_weight: float32 [768, 768], P('head'), may hold values from -4 to 4
- expand_weight: float32 [768, 3072], P(None, 'head'), may hold values from -0.21875 to 0.21875
- shrink_weight: float32 [3072, 768], P('head'), may hold values from -0.109375 to 0.109375
- gain_moment: float32 [2, 768], replicated, may hold values from 409.6 to 8192
- heads_rows: float32 [768], P('batch'), may hold values from 655.36 to 5734.4
- heads_cols: float32 [3, 768], P(None, 'head'), may hold values from 655.36 to 5734.4
- merge_rows: float32 [768], P('head'), may hold values from 1.92 to 16
- merge_cols: float32 [768], P('batch'), may hold values from 1.92 to 16
- expand_rows: float32 [768], P('batch'), may hold values from 57.344 to 491.52
- expand_cols: float32 [3072], P('head'), may hold values from 57.344 to 491.52
- shrink_rows: float32 [3072], P('head'), may hold values from 245.76 to 2293.76
- shrink_cols: float32 [768], P('batch'), may hold values from 245.76 to 2293.76
Outputs:
- block_out: float32 [8192, 768], P('batch')
- residual_grad: float32 [8192, 768], P('batch')
- heads_grad: float32 [768, 3, 768], P('batch', None, 'head')
- heads_rows_next: float32 [768], P('batch')
- heads_cols_next: float32 [3, 768], P(None, 'head')
- heads_weight_next: float32 [768, 3, 768], P('batch', None, 'head')
- merge_grad: float32 [768, 768], P('head', 'batch')
- merge_rows_next: float32 [768], P('head')
- merge_cols_next: float32 [768], P('batch')
- merge_weight_next: float32 [768, 768], P('head', 'batch')
- expand_grad: float32 [768, 3072], P('batch', 'head')
- expand_rows_next: float32 [768], P('batch')
- expand_cols_next: float32 [3072], P('head')
- expand_weight_next: float32 [768, 3072], P('batch', 'head')
- shrink_grad: float32 [3072, 768], P('head', 'batch')
- shrink_rows_next: float32 [3072], P('head')
- shrink_cols_next: float32 [768], P('batch')
- shrink_weight_next: float32 [3072, 768], P('head', 'batch')
- gains_grad: float32 [2, 768], replicated
- gain_moment_next: float32 [2, 768], replicated
- gains_next: float32 [2, 768], replicated
- update_rms: float32 [], replicated
Inputs may be any that keep to these rules, and one draw needn't show every extreme that they name: Live lengths of the sequences; one sequence, drawn from the seed, is full.
All inputs are finite; a program needn't handle non-finite values.
Results may differ from a plain program's by a relative error of at most 0.012.
The roundings to bfloat16 on the way count: a program that leaves them out, or rounds other values in their place, can miss the bound.
Values sent between devices are 32-bit elements; how exact they have to be, the bound alone decides.
A program may use at most 128 MiB of HBM per device.

v0:
```python
from functools import partial

import jax
import jax.numpy as jnp
from jax import lax
from jax.sharding import PartitionSpec as P

HEAD_DIM = 64
FF = 3072
STEP = 10


tiny_term = 1e-30
clip_level = 0.5


def layer_norm(values, gain):
    center = values - jnp.mean(values, -1, keepdims=True)
    inv_dev = lax.rsqrt(jnp.mean(center * center, -1, keepdims=True) + 1e-05)
    normed = center * inv_dev
    return (normed * gain, normed, inv_dev)


def norm_back(upstream, gain, normed, inv_dev):
    scaled = upstream * gain
    inner = (
        scaled
        - jnp.mean(scaled, -1, keepdims=True)
        - normed * jnp.mean(scaled * normed, -1, keepdims=True)
    )
    return (inner * inv_dev, jnp.sum(upstream * normed, 0))


def score_block(query_blk, key_rows, block_start, length, positions, score_scale):
    scores = (
        jnp.einsum("qhd,khd->hqk", query_blk, key_rows, preferred_element_type=jnp.float32)
        * score_scale
    )
    row_index = block_start + jnp.arange(query_blk.shape[0], dtype=jnp.int32)
    allowed = (positions[None, :] <= row_index[:, None]) & (positions[None, :] < length)
    soft_abs = jnp.sqrt(scores * scores + 1.0)
    masked = jnp.where(allowed[None], soft_abs, -jnp.inf)
    return (scores, soft_abs, masked)


def spread(piece, start_at, full_len, along):
    extent = list(piece.shape)
    extent[along] = full_len
    return lax.dynamic_update_slice_in_dim(
        jnp.zeros(tuple(extent), jnp.float32), piece, start_at, along
    )


def factored(
    gradient, row_sq, col_sq, row_old, col_old, row_total, old_total, row_len, col_len, decay_rate
):
    row_next = decay_rate * row_old + (1.0 - decay_rate) * (row_sq / col_len + tiny_term)
    col_next = decay_rate * col_old + (1.0 - decay_rate) * (col_sq / row_len + tiny_term)
    row_mean = decay_rate * old_total / row_len + (1.0 - decay_rate) * (
        row_total / (row_len * col_len) + tiny_term
    )
    update = gradient * lax.rsqrt(row_next[:, None] * col_next[None, :] / row_mean)
    return (row_next, col_next, update)


def body(
    residual,
    cotangent,
    lengths,
    gains,
    heads_weight,
    merge_weight,
    expand_weight,
    shrink_weight,
    gain_moment,
    heads_rows,
    heads_cols,
    merge_rows,
    merge_cols,
    expand_rows,
    expand_cols,
    shrink_rows,
    shrink_cols,
):
    seq_len, model_width = residual.shape
    local_width = merge_weight.shape[0]
    local_heads = local_width // HEAD_DIM
    local_ff = expand_weight.shape[1]
    block_rows = min(512, seq_len)
    block_count = seq_len // block_rows
    score_scale = HEAD_DIM ** (-0.5)
    length = lengths[0]
    positions = jnp.arange(seq_len, dtype=jnp.int32)
    live_rows = (positions < length).astype(jnp.float32)
    heads_low = heads_weight.astype(jnp.bfloat16).reshape(model_width, 3 * local_width)
    merge_low = merge_weight.astype(jnp.bfloat16)
    expand_low = expand_weight.astype(jnp.bfloat16)
    shrink_low = shrink_weight.astype(jnp.bfloat16)
    normed_in, normed_one, inv_one = layer_norm(residual, gains[0])
    first_low = normed_in.astype(jnp.bfloat16)
    joint_rows = jnp.dot(first_low, heads_low, preferred_element_type=jnp.float32).astype(
        jnp.bfloat16
    )
    joint_rows = joint_rows.reshape(seq_len, 3, local_heads, HEAD_DIM)
    queries = joint_rows[:, 0]
    key_rows = joint_rows[:, 1]
    value_rows = joint_rows[:, 2]
    query_blocks = queries.reshape(block_count, block_rows, local_heads, HEAD_DIM)
    starts = jnp.arange(block_count, dtype=jnp.int32) * block_rows

    def forward_block(block_pair):
        query_blk, block_start = block_pair
        scores, soft_abs, masked = score_block(
            query_blk, key_rows, block_start, length, positions, score_scale
        )
        row_top = jnp.max(masked, -1, keepdims=True)
        exponent = jnp.exp(masked - row_top)
        row_total = jnp.sum(exponent, -1, keepdims=True)
        probs = (jnp.tanh(scores) * (exponent / row_total)).astype(jnp.bfloat16)
        mixed = jnp.einsum("hqk,khd->qhd", probs, value_rows, preferred_element_type=jnp.float32)
        return (mixed.astype(jnp.bfloat16), row_top + jnp.log(row_total))

    attended, logsums = lax.map(forward_block, (query_blocks, starts))
    attended = attended.reshape(seq_len, local_width)
    attn_total = lax.psum(jnp.dot(attended, merge_low, preferred_element_type=jnp.float32), "head")
    middle = residual + attn_total
    normed_mid, normed_two, inv_two = layer_norm(middle, gains[1])
    second_low = normed_mid.astype(jnp.bfloat16)
    expanded = jnp.dot(second_low, expand_low, preferred_element_type=jnp.float32)
    activated = jax.nn.gelu(expanded, approximate=True).astype(jnp.bfloat16)
    mlp_total = lax.psum(jnp.dot(activated, shrink_low, preferred_element_type=jnp.float32), "head")
    block_out = middle + mlp_total
    out_grad = cotangent * live_rows[:, None]
    out_low = out_grad.astype(jnp.bfloat16)
    shrink_local = jnp.einsum("tf,td->fd", activated, out_low, preferred_element_type=jnp.float32)
    act_grad = jnp.einsum("td,fd->tf", out_low, shrink_low, preferred_element_type=jnp.float32)
    _, gelu_pull = jax.vjp(partial(jax.nn.gelu, approximate=True), expanded)
    expand_back = gelu_pull(act_grad)[0].astype(jnp.bfloat16)
    expand_local = jnp.einsum(
        "td,tf->df", second_low, expand_back, preferred_element_type=jnp.float32
    )
    mid_part = jnp.einsum("tf,df->td", expand_back, expand_low, preferred_element_type=jnp.float32)
    mid_norm_grad = lax.psum(mid_part, "head")
    mid_back, gain_two = norm_back(mid_norm_grad, gains[1], normed_two, inv_two)
    middle_grad = out_grad + mid_back
    middle_low = middle_grad.astype(jnp.bfloat16)
    merge_local = jnp.einsum("tc,td->cd", attended, middle_low, preferred_element_type=jnp.float32)
    attended_back = jnp.einsum(
        "td,cd->tc", middle_low, merge_low, preferred_element_type=jnp.float32
    ).astype(jnp.bfloat16)
    back_blocks = attended_back.reshape(block_count, block_rows, local_heads, HEAD_DIM)

    def backward_block(running, block_item):
        key_sum, value_sum = running
        query_blk, back_blk, logsum, block_start = block_item
        scores, soft_abs, masked = score_block(
            query_blk, key_rows, block_start, length, positions, score_scale
        )
        weights = jnp.exp(masked - logsum)
        tangent = jnp.tanh(scores)
        probs = tangent * weights
        value_sum = value_sum + jnp.einsum(
            "hqk,qhd->khd", probs.astype(jnp.bfloat16), back_blk, preferred_element_type=jnp.float32
        )
        prob_grad = jnp.einsum(
            "qhd,khd->hqk", back_blk, value_rows, preferred_element_type=jnp.float32
        )
        row_dot = jnp.sum(probs * prob_grad, -1, keepdims=True)
        score_back = (
            (1.0 - tangent * tangent) * weights * prob_grad
            + scores / soft_abs * weights * (tangent * prob_grad - row_dot)
        ).astype(jnp.bfloat16)
        query_back = (
            jnp.einsum("hqk,khd->qhd", score_back, key_rows, preferred_element_type=jnp.float32)
            * score_scale
        )
        key_sum = (
            key_sum
            + jnp.einsum("hqk,qhd->khd", score_back, query_blk, preferred_element_type=jnp.float32)
            * score_scale
        )
        return ((key_sum, value_sum), query_back)

    empty = jnp.zeros((seq_len, local_heads, HEAD_DIM), jnp.float32)
    (key_back, value_back), query_back = lax.scan(
        backward_block, (empty, empty), (query_blocks, back_blocks, logsums, starts)
    )
    joint_back = jnp.stack(
        [query_back.reshape(seq_len, local_heads, HEAD_DIM), key_back, value_back], 1
    )
    joint_back = joint_back.astype(jnp.bfloat16).reshape(seq_len, 3 * local_width)
    heads_local = jnp.einsum(
        "td,tc->dc", first_low, joint_back, preferred_element_type=jnp.float32
    ).reshape(model_width, 3, local_width)
    in_part = jnp.einsum("tc,dc->td", joint_back, heads_low, preferred_element_type=jnp.float32)
    in_norm_grad = lax.psum(in_part, "head")
    in_back, gain_one = norm_back(in_norm_grad, gains[0], normed_one, inv_one)
    residual_grad = middle_grad + in_back
    batch_count = lax.axis_size("batch")
    head_count = lax.axis_size("head")
    batch_pos = lax.axis_index("batch")
    head_pos = lax.axis_index("head")
    row_share = model_width // batch_count
    row_off = batch_pos * row_share
    head_off = head_pos * local_width
    ff_off = head_pos * local_ff
    gradients = (heads_local, merge_local, expand_local, shrink_local)
    summed = lax.psum((gradients[0], gradients[1], gradients[2], gradients[3]), "batch")
    heads_own = lax.dynamic_slice_in_dim(summed[0], row_off, row_share, 0)
    merge_own = lax.dynamic_slice_in_dim(summed[1], row_off, row_share, 1)
    expand_own = lax.dynamic_slice_in_dim(summed[2], row_off, row_share, 0)
    shrink_own = lax.dynamic_slice_in_dim(summed[3], row_off, row_share, 1)
    heads_master = lax.dynamic_slice_in_dim(heads_weight, row_off, row_share, 0)
    merge_master = lax.dynamic_slice_in_dim(merge_weight, row_off, row_share, 1)
    expand_master = lax.dynamic_slice_in_dim(expand_weight, row_off, row_share, 0)
    shrink_master = lax.dynamic_slice_in_dim(shrink_weight, row_off, row_share, 1)
    heads_sq = heads_own * heads_own
    merge_sq = merge_own * merge_own
    expand_sq = expand_own * expand_own
    shrink_sq = shrink_own * shrink_own
    scalars = jnp.stack(
        [
            jnp.sum(heads_master * heads_master),
            jnp.sum(merge_master * merge_master),
            jnp.sum(expand_master * expand_master),
            jnp.sum(shrink_master * shrink_master),
            jnp.sum(heads_rows) / head_count,
            jnp.sum(merge_rows) / batch_count,
            jnp.sum(expand_rows) / head_count,
            jnp.sum(shrink_rows) / batch_count,
        ]
    )
    gain_part = jnp.stack([gain_one, gain_two]) / head_count
    statistics = lax.psum(
        (
            spread(jnp.sum(heads_sq, (1, 2)), row_off, model_width, 0),
            spread(jnp.sum(heads_sq, 0), head_off, model_width, 1),
            spread(jnp.sum(merge_sq, 1), head_off, model_width, 0),
            spread(jnp.sum(merge_sq, 0), row_off, model_width, 0),
            spread(jnp.sum(expand_sq, 1), row_off, model_width, 0),
            spread(jnp.sum(expand_sq, 0), ff_off, FF, 0),
            spread(jnp.sum(shrink_sq, 1), ff_off, FF, 0),
            spread(jnp.sum(shrink_sq, 0), row_off, model_width, 0),
            scalars,
            gain_part,
        ),
        ("batch", "head"),
    )
    totals = statistics[8]
    decay_rate = 1.0 - STEP ** (-0.8)
    heads_rows_next, heads_cols_flat, heads_update = factored(
        heads_own.reshape(row_share, 3 * local_width),
        lax.dynamic_slice_in_dim(statistics[0], row_off, row_share, 0),
        lax.dynamic_slice_in_dim(statistics[1], head_off, local_width, 1).reshape(3 * local_width),
        heads_rows,
        heads_cols.reshape(3 * local_width),
        jnp.sum(statistics[0]),
        totals[4],
        model_width,
        3 * model_width,
        decay_rate,
    )
    merge_rows_next, merge_cols_next, merge_update = factored(
        merge_own,
        lax.dynamic_slice_in_dim(statistics[2], head_off, local_width, 0),
        lax.dynamic_slice_in_dim(statistics[3], row_off, row_share, 0),
        merge_rows,
        merge_cols,
        jnp.sum(statistics[2]),
        totals[5],
        model_width,
        model_width,
        decay_rate,
    )
    expand_rows_next, expand_cols_next, expand_update = factored(
        expand_own,
        lax.dynamic_slice_in_dim(statistics[4], row_off, row_share, 0),
        lax.dynamic_slice_in_dim(statistics[5], ff_off, local_ff, 0),
        expand_rows,
        expand_cols,
        jnp.sum(statistics[4]),
        totals[6],
        model_width,
        FF,
        decay_rate,
    )
    shrink_rows_next, shrink_cols_next, shrink_update = factored(
        shrink_own,
        lax.dynamic_slice_in_dim(statistics[6], ff_off, local_ff, 0),
        lax.dynamic_slice_in_dim(statistics[7], row_off, row_share, 0),
        shrink_rows,
        shrink_cols,
        jnp.sum(statistics[6]),
        totals[7],
        FF,
        model_width,
        decay_rate,
    )
    heads_update = heads_update.reshape(row_share, 3, local_width)
    gains_grad = statistics[9]
    gain_moment_next = decay_rate * gain_moment + (1.0 - decay_rate) * (
        gains_grad * gains_grad + tiny_term
    )
    gain_step = gains_grad * lax.rsqrt(gain_moment_next)
    local_squares = (
        jnp.sum(heads_update * heads_update)
        + jnp.sum(merge_update * merge_update)
        + jnp.sum(expand_update * expand_update)
        + jnp.sum(shrink_update * shrink_update)
    )
    squares = lax.psum(local_squares, ("batch", "head")) + jnp.sum(gain_step * gain_step)
    param_count = 4.0 * model_width * model_width + 2.0 * model_width * FF + 2.0 * model_width
    update_rms = jnp.sqrt(squares / param_count)
    clip = 1.0 / jnp.maximum(1.0, update_rms / clip_level)
    heads_weight_next = (
        heads_master - jnp.sqrt(totals[0] / (3.0 * model_width * model_width)) * clip * heads_update
    )
    merge_weight_next = (
        merge_master - jnp.sqrt(totals[1] / (1.0 * model_width * model_width)) * clip * merge_update
    )
    expand_weight_next = (
        expand_master - jnp.sqrt(totals[2] / (1.0 * model_width * FF)) * clip * expand_update
    )
    shrink_weight_next = (
        shrink_master - jnp.sqrt(totals[3] / (1.0 * FF * model_width)) * clip * shrink_update
    )
    gains_next = gains - jnp.sqrt(jnp.mean(gains * gains, 1, keepdims=True)) * clip * gain_step
    return (
        block_out,
        residual_grad,
        heads_own,
        heads_rows_next,
        heads_cols_flat.reshape(3, local_width),
        heads_weight_next,
        merge_own,
        merge_rows_next,
        merge_cols_next,
        merge_weight_next,
        expand_own,
        expand_rows_next,
        expand_cols_next,
        expand_weight_next,
        shrink_own,
        shrink_rows_next,
        shrink_cols_next,
        shrink_weight_next,
        gains_grad,
        gain_moment_next,
        gains_next,
        update_rms,
    )


def solution(mesh):
    return jax.shard_map(
        body,
        mesh=mesh,
        in_specs=(
            P("batch", None),
            P("batch", None),
            P("batch"),
            P(),
            P(None, None, "head"),
            P("head", None),
            P(None, "head"),
            P("head", None),
            P(),
            P("batch"),
            P(None, "head"),
            P("head"),
            P("batch"),
            P("batch"),
            P("head"),
            P("head"),
            P("batch"),
        ),
        out_specs=(
            P("batch", None),
            P("batch", None),
            P("batch", None, "head"),
            P("batch"),
            P(None, "head"),
            P("batch", None, "head"),
            P("head", "batch"),
            P("head"),
            P("batch"),
            P("head", "batch"),
            P("batch", "head"),
            P("batch"),
            P("head"),
            P("batch", "head"),
            P("head", "batch"),
            P("head"),
            P("batch"),
            P("head", "batch"),
            P(),
            P(),
            P(),
            P(),
        ),
        check_vma=False,
    )
```

profile of v0, /device:TPU:0, one launch (start us, length us, event | category | flops | bytes accessed | tf_op | source)
XLA Modules:
  0.0 827.6 jit_solution(10120781854315290330)
XLA Ops:
  7.3 2.3 reduce_sum.342
  13.6 2.1 reshape_squeeze.3
  15.6 1.8 copy.43
  17.4 36.7 %while.30 = (s32[]{:T(128)}, bf16[2,512,3,64]{1,3,2,0:T(8,128)(2,1)}, f32[2,3,512,1]{2,1,3,0:T(4,128)}, bf16[2,512,3,64]{1,3,2,0:T(8,128)(2,1)}, bf16[1024,3,64]...) while((s32[]{:T(128)}, ...), condition=%wide.region_5.6_spmd.clone.clone, body=%wide.region_2.5_spmd.clone.clone.sunk | while | flops 433684480 | bytes 26931416 | solution.py:123
  19.7 5.4 fusion.143
  25.2 4.3 fusion.144
  29.5 5.5 fusion.145
  38.1 5.4 fusion.143
  43.5 4.3 fusion.144
  47.8 5.5 fusion.145
  56.3 3.4 fusion.91
  60.7 70.3 %all-reduce.9.cloned.1.call-done = f32[1024,768]{1,0:T(8,128)} async-done(((f32[1024,768]{1,0:T(8,128)}), f32[1024,768]{1,0:T(8,128)}) %all-reduce.9.cloned.1.call-update) | async-done | bytes 3145744 | tf_op jit(solution)/shard_map/psum | solution.py:125
  131.0 2.3 fusion.96
  133.9 2.2 copy-done.33
  138.7 3.3 fusion.74
  143.2 3.1 fusion.86
  146.5 6.4 fusion.82
  152.9 62.2 %all-reduce.11.cloned.1.call-done = f32[1024,768]{1,0:T(8,128)} async-done(((f32[1024,768]{1,0:T(8,128)}), f32[1024,768]{1,0:T(8,128)}) %all-reduce.11.cloned.1.call-update) | async-done | bytes 3145744 | tf_op jit(solution)/shard_map/psum | solution.py:143
  215.1 3.6 multiply_reduce_fusion.1
  223.7 99.6 %while.31 = (s32[]{:T(128)}, f32[1024,3,64]{0,2,1:T(8,128)}, f32[1024,3,64]{0,2,1:T(8,128)}, bf16[2,512,3,64]{1,0,3,2:T(2,128)(2,1)}, bf16[2,512,3,64]{1,3,2,0:T...) while((s32[]{:T(128)}, f32[1024,3,64]{0,2,1:T(8,128)}, ...), condition=%wide.region_15.16_spmd.clone.clone, body=%wide.region_13.15_spmd.clone.clone.sunk | while | flops 1257377792 | bytes 76981536 | solution.py:185
  237.1 2.1 fusion.160
  239.2 2.7 copy-done
  241.9 6.8 fusion.163
  248.7 18.2 %add_convert_fusion.2 = bf16[3,512,1024]{2,1,0:T(8,128)(2,1)S(1)} fusion(f32[3,512,1024]{2,1,0:T(8,128)} %copy-done, f32[3,512]{1,0:T(4,128)S(1)} %dynamic-slice_bitcast_fusion.2, pred[512,1024]{1,0:T(8,128)(4,1)} %copy-done.11, bf16[1024,3,64]{0,2,1:T(8,128)(2,1)} %get-tuple-element.558, bf16[2,512,3,64]{1,3,2,0:T(8,128)(2,1)} %get-tuple-element.557, ...), kind=kOutput, calls=%fused_computation.24.clone.1 | convolution fusion | flops 438831616 | bytes 17974272 | tf_op jit(solution)/shard_map/while/body/eval_jaxpr/sub | solution.py:171
  270.9 7.5 dynamic_update_slice.57
  281.5 2.1 fusion.160
  283.6 2.7 copy-done
  286.3 7.1 fusion.163
  293.4 18.1 %add_convert_fusion.2 = bf16[3,512,1024]{2,1,0:T(8,128)(2,1)S(1)} fusion(f32[3,512,1024]{2,1,0:T(8,128)} %copy-done, f32[3,512]{1,0:T(4,128)S(1)} %dynamic-slice_bitcast_fusion.2, pred[512,1024]{1,0:T(8,128)(4,1)} %copy-done.11, bf16[1024,3,64]{0,2,1:T(8,128)(2,1)} %get-tuple-element.558, bf16[2,512,3,64]{1,3,2,0:T(8,128)(2,1)} %get-tuple-element.557, ...), kind=kOutput, calls=%fused_computation.24.clone.1 | convolution fusion | flops 438831616 | bytes 17974272 | tf_op jit(solution)/shard_map/while/body/eval_jaxpr/sub | solution.py:171
  315.6 7.5 dynamic_update_slice.57
  327.3 3.1 fusion.98
  330.5 1.8 copy-done.5
  332.3 4.6 fusion.95
  337.0 3.3 fusion.94
  342.4 3.3 fusion.75
  351.4 1.9 constant_dynamic-slice_fusion.4
  354.4 2.1 constant_dynamic-slice_fusion.3
  356.5 1.9 copy.56
  364.0 2.7 stack.56
  366.8 83.7 %all-reduce.15.cloned.1.call-done = (f32[1024,768]{1,0:T(8,128)}, f32[1024,768]{1,0:T(8,128)}) async-done(((f32[1024,768]{1,0:T(8,128)}, f32[1024,768]{1,0:T(8,128)}), (f32[1024,768]{1,0:T(8,128)}, f32[1024,768]{1,0:T(8,128)})) %all-reduce.15.cloned.1.call-update) | async-done | bytes 6291472 | tf_op jit(solution)/shard_map/psum | solution.py:131
  450.5 5.0 add.275
  455.5 1.7 multiply_reduce_fusion.2
  457.4 2.4 multiply_add_fusion
  459.9 247.1 %all-reduce.13.cloned.1.call-done = (f32[768,3,192]{2,0,1:T(8,128)}, f32[192,768]{1,0:T(8,128)}, f32[768,768]{1,0:T(8,128)}, f32[768,768]{0,1:T(8,128)}) async-done(((f32[768,3,192]{2,0,1:T(8,128)}, f32[192,768]{1,0:T(8,128)}, f32[768,768]{1,0:T(8,128)}, f32[768,768]{0,1:T(8,128)}), (f32[768,3,192]{2,0,1:T(8,128)}, f32[192,768]{1,0:T(8,128)}, f32[768,768]{1,0:T(8,128)}, ...) | async-done | bytes 7077904 | tf_op jit(solution)/shard_map/psum | solution.py:208
  713.7 40.2 %all-reduce.1 = (f32[768]{0:T(1024)S(1)}, f32[3,768]{1,0:T(4,128)S(1)}, f32[8]{0:T(128)S(1)}, f32[768]{0:T(1024)S(1)}, f32[768]{0:T(1024)S(1)}, /*index=5*/f32[7...) all-reduce(f32[768]{0:T(1024)S(1)} %dynamic_update_slice.36, ...), channel_id=1, replica_groups=mesh['batch'=8,'head'=4] {'batch','head'}, use_global_device_ids=true, to_apply=%region_21.22 | all-reduce | flops 12296 | bytes 98368 | tf_op jit(solution)/shard_map/psum | solution.py:234
  771.3 40.2 %all-reduce = (f32[]{:T(128)}, f32[2,768]{1,0:T(2,128)S(1)}) all-reduce(f32[]{:T(128)S(6)} %add.309, f32[2,768]{1,0:T(2,128)S(1)} %maximum_multiply_fusion), channel_id=1, replica_groups=mesh['batch'=8,'head'=4] {'batch','head'}, use_global_device_ids=true, to_apply=%region_56.57 | all-reduce | flops 1537 | bytes 12296 | tf_op jit(solution)/shard_map/psum | solution.py:311
  815.2 1.7 multiply_subtract_fusion.3
  816.9 1.8 multiply_subtract_fusion.1
  (281 shorter events, 68.4 us)
Async XLA Ops:
  7.2 123.8 %all-reduce.9.cloned.1.call-start = ((), (), s32[]{:S(2)}) async-start(), calls=%async_computation | async-start | bytes 6291456 | tf_op jit(solution)/shard_map/psum | solution.py:125
  11.2 207.6 %copy-start.43 = (f32[768]{0:T(1024)}, f32[768]{0:T(1024)S(1)}, u32[]{:S(2)}) copy-start(f32[768]{0:T(1024)S(1)} %get-tuple-element.295) | copy-start | bytes 9220
  25.1 4.3 copy-start.30
  25.1 4.3 copy-start.31
  43.5 4.3 copy-start.30
  43.5 4.3 copy-start.31
  54.1 5.6 copy-start.71
  59.7 155.4 %all-reduce.11.cloned.1.call-start = ((), (), s32[]{:S(2)}) async-start(), calls=%async_computation.1 | async-start | bytes 6291456 | tf_op jit(solution)/shard_map/psum | solution.py:143
  60.7 158.0 %copy-start.55 = (f32[1024]{0:T(1024)}, f32[1024]{0:T(1024)S(1)}, u32[]{:S(2)}) copy-start(f32[1024]{0:T(1024)S(1)} %fusion.93) | copy-start | bytes 12292
  133.3 4.3 copy-start.3
  133.3 85.4 %copy-start.36 = (f32[1024]{0:T(1024)}, f32[1024]{0:T(1024)S(1)}, u32[]{:S(2)}) copy-start(f32[1024]{0:T(1024)S(1)} %broadcast_multiply_fusion.4) | copy-start | bytes 12292
  133.9 84.9 %copy-start.50 = (f32[1024]{0:T(1024)}, f32[1024]{0:T(1024)S(1)}, u32[]{:S(2)}) copy-start(f32[1024]{0:T(1024)S(1)} %add_rsqrt_fusion) | copy-start | bytes 12292
  146.4 304.1 %all-reduce.15.cloned.1.call-start = ((), (), s32[]{:S(2)}) async-start(), calls=%async_computation.3 | async-start | bytes 12582912 | tf_op jit(solution)/shard_map/psum | solution.py:131
  146.5 68.6 %copy-start.4 = (f32[1024,768]{1,0:T(8,128)S(1)}, f32[1024,768]{1,0:T(8,128)}, u32[]{:S(2)}) copy-start(f32[1024,768]{1,0:T(8,128)} %copy-done.3) | copy-start | bytes 9437188
  215.1 3.6 copy-start.13
  215.1 3.8 copy-start.18
  323.3 4.0 copy-start.29
  330.4 6.5 copy-start.56
  330.4 376.6 %all-reduce.13.cloned.1.call-start = ((), (), s32[]{:S(2)}) async-start(), calls=%async_computation.2 | async-start | bytes 15335424 | tf_op jit(solution)/shard_map/psum | solution.py:208
  332.3 4.7 copy-start.19
  332.3 4.7 copy-start.74
  336.9 3.3 copy-start.7
  337.0 3.3 copy-start.15
  337.0 4.7 copy-start.26
  345.7 4.5 copy-start.68
  345.7 20.9 %copy-start.40 = (f32[2,768]{1,0:T(2,128)S(1)}, f32[2,768]{1,0:T(2,128)}, u32[]{:S(2)}) copy-start(f32[2,768]{1,0:T(2,128)} %param.24) | copy-start | bytes 18436
  345.7 21.0 %copy-start.54 = (f32[768]{0:T(1024)S(1)}, f32[768]{0:T(1024)}, u32[]{:S(2)}) copy-start(f32[768]{0:T(1024)} %get-tuple-element.283) | copy-start | bytes 9220
  450.5 5.0 copy-start.12
  457.4 307.2 %copy-start.64 = (f32[3,192]{1,0:T(4,128)S(1)}, f32[3,192]{1,0:T(4,128)}, u32[]{:S(2)}) copy-start(f32[3,192]{1,0:T(4,128)} %param.31) | copy-start | bytes 6916
  457.4 307.3 %copy-start.69 = (f32[96]{0:T(128)S(1)}, f32[96]{0:T(128)}, u32[]{:S(2)}) copy-start(f32[96]{0:T(128)} %param.33) | copy-start | bytes 1156
  457.4 307.4 %copy-start.70 = (f32[96]{0:T(128)S(1)}, f32[96]{0:T(128)}, u32[]{:S(2)}) copy-start(f32[96]{0:T(128)} %param.37) | copy-start | bytes 1156
  457.4 307.4 %copy-start.65 = (f32[768]{0:T(1024)S(1)}, f32[768]{0:T(1024)}, u32[]{:S(2)}) copy-start(f32[768]{0:T(1024)} %param.35) | copy-start | bytes 9220
  459.9 351.6 %copy-start.59 = (f32[2,768]{1,0:T(2,128)S(1)}, f32[2,768]{1,0:T(2,128)}, u32[]{:S(2)}) copy-start(f32[2,768]{1,0:T(2,128)} %param.29) | copy-start | bytes 18436
  459.9 354.5 %copy-start.23 = (f32[768,96]{0,1:T(8,128)S(1)}, f32[768,96]{0,1:T(8,128)}, u32[]{:S(2)}) copy-start(f32[768,96]{0,1:T(8,128)} %copy.56) | copy-start | bytes 884740
  708.1 111.2 %copy-start.21 = (f32[96,3,192]{2,0,1:T(8,128)}, f32[96,3,192]{2,0,1:T(8,128)S(1)}, u32[]{:S(2)}) copy-start(f32[96,3,192]{2,0,1:T(8,128)S(1)} %get-tuple-element.357) | copy-start | bytes 663556
  709.4 110.0 %copy-start.27 = (f32[192,96]{1,0:T(8,128)}, f32[192,96]{1,0:T(8,128)S(1)}, u32[]{:S(2)}) copy-start(f32[192,96]{1,0:T(8,128)S(1)} %get-tuple-element.356) | copy-start | bytes 221188
  710.5 108.8 %copy-start.20 = (f32[96,768]{1,0:T(8,128)}, f32[96,768]{1,0:T(8,128)S(1)}, u32[]{:S(2)}) copy-start(f32[96,768]{1,0:T(8,128)S(1)} %get-tuple-element.355) | copy-start | bytes 884740
  711.8 107.6 %copy-start.22 = (f32[768,96]{0,1:T(8,128)}, f32[768,96]{0,1:T(8,128)S(1)}, u32[]{:S(2)}) copy-start(f32[768,96]{0,1:T(8,128)S(1)} %get-tuple-element.354) | copy-start | bytes 884740
  754.0 65.3 %copy-start.45 = (f32[768]{0:T(1024)}, f32[768]{0:T(1024)S(1)}, u32[]{:S(2)}) copy-start(f32[768]{0:T(1024)S(1)} %multiply_add_fusion.3) | copy-start | bytes 9220
  754.7 64.6 %copy-start.60 = (f32[96]{0:T(128)}, f32[96]{0:T(128)S(1)}, u32[]{:S(2)}) copy-start(f32[96]{0:T(128)S(1)} %multiply_add_fusion.8) | copy-start | bytes 1156
  756.7 62.7 %copy-start.58 = (f32[192]{0:T(256)}, f32[192]{0:T(256)S(1)}, u32[]{:S(2)}) copy-start(f32[192]{0:T(256)S(1)} %multiply_add_fusion.6) | copy-start | bytes 2308
  758.0 61.3 %copy-start.61 = (f32[96]{0:T(128)}, f32[96]{0:T(128)S(1)}, u32[]{:S(2)}) copy-start(f32[96]{0:T(128)S(1)} %multiply_add_fusion.10) | copy-start | bytes 1156
  764.7 54.7 %copy-start.46 = (f32[3,192]{1,0:T(4,128)}, f32[3,192]{1,0:T(4,128)S(1)}, u32[]{:S(2)}) copy-start(f32[3,192]{1,0:T(4,128)S(1)} %multiply_add_fusion.5) | copy-start | bytes 6916
  764.8 54.7 %copy-start.62 = (f32[96]{0:T(128)}, f32[96]{0:T(128)S(1)}, u32[]{:S(2)}) copy-start(f32[96]{0:T(128)S(1)} %multiply_add_fusion.9) | copy-start | bytes 1156
  764.8 54.6 %copy-start.63 = (f32[96]{0:T(128)}, f32[96]{0:T(128)S(1)}, u32[]{:S(2)}) copy-start(f32[96]{0:T(128)S(1)} %multiply_add_fusion.7) | copy-start | bytes 1156
  764.9 54.5 %copy-start.47 = (f32[768]{0:T(1024)}, f32[768]{0:T(1024)S(1)}, u32[]{:S(2)}) copy-start(f32[768]{0:T(1024)S(1)} %multiply_add_fusion.4) | copy-start | bytes 9220
  811.5 8.0 copy-start.52
  812.1 7.4 copy-start.53
  (39 other events, 74.0 us)
Sparse Core Ops, SparseCore 0:
  59.8 71.1 all-reduce.8
  146.5 68.5 all-reduce.10
  330.5 119.8 all-reduce.14
  454.8 252.1 all-reduce.12
where the time goes:
time: 839 us; the launch traced here: 828 us
  waiting for transfers between devices  463 us (55%)
  matrix products  117 us (14%)
  blocking collectives  80.4 us (10%)
  other arithmetic  63.6 us (8%)
  local copies, waits for them, and re-layouts  60.2 us (7%)
  between operations  31.4 us (4%)
  loops' own time  10.8 us (1%)
    psum x1, waiting for transfers between devices, body(): lax.psum((gradients[0], gradients[1], gradients[2], gradients[3]), 'batch')  247 us
    psum x1, waiting for transfers between devices, body(): lax.psum(jnp.dot(activated, shrink_low, preferred_element_type=jnp.float3...  83.7 us
    psum x1, waiting for transfers between devices, body(): lax.psum(jnp.dot(attended, merge_low, preferred_element_type=jnp.float32)...  70.3 us
    psum x1, waiting for transfers between devices, body(): mid_norm_grad = lax.psum(mid_part, 'head')  62.2 us
    psum x1, blocking collectives, body(): lax.psum((spread(jnp.sum(heads_sq, (1, 2)), row_off, model_width, 0), spr...  40.2 us
    psum x1, blocking collectives, body(): lax.psum(local_squares, ('batch', 'head')) + jnp.sum(gain_step * gain_step)  40.2 us
    sub x2, matrix products, backward_block(): tangent * prob_grad - row_dot  36.4 us
    unnamed x143, local copies, waits for them, and re-layouts  18.2 us
  transfers between devices with their start and end apart: 4, of which 4 were waited for; matrix products, arithmetic and copies ran while one was open for 6% of the time, Pallas kernels for 0%

commit v1 on v0

v1 whole, which is shorter than its diff:
```python
from functools import partial

import jax
import jax.numpy as jnp
from jax import lax
from jax.experimental import pallas as pl
from jax.experimental.pallas import tpu as pltpu
from jax.sharding import PartitionSpec as P

HEAD_DIM = 64
FF = 3072
STEP = 10
CHUNK = 256

tiny_term = 1e-30
clip_level = 0.5
f32 = jnp.float32
bf16 = jnp.bfloat16
LOG2E = 1.4426950408889634
GELU_A = 0.7978845608028654
GELU_B = 0.044715
MESH = pl.DeviceIdType.MESH
VMEM_LIMIT = 63 * 1024 * 1024


def mm(a, b):
    return jnp.dot(a, b, preferred_element_type=f32)


def mm_nt(a, b):
    return lax.dot_general(a, b, (((1,), (1,)), ((), ())), preferred_element_type=f32)


def mm_tn(a, b):
    return lax.dot_general(a, b, (((0,), (0,)), ((), ())), preferred_element_type=f32)


def identity(size):
    rows = lax.broadcasted_iota(jnp.int32, (size, size), 0)
    return (rows == lax.broadcasted_iota(jnp.int32, (size, size), 1)).astype(bf16)


def band(start, size):
    return pl.ds(pl.multiple_of(start, size), size)


def tiles(total, rows, body):
    def step(i, carry):
        body(i * rows)
        return carry

    lax.fori_loop(0, total // rows, step, 0)


def cast_rows(src, dst, rows=64):
    def one(at):
        dst[band(at, rows), :] = src[band(at, rows), :].astype(bf16)

    tiles(src.shape[0], rows, one)


def fold(values, how):
    groups = values.reshape(values.shape[0] // 8, 8, values.shape[1])
    return how(groups, 0)


def normalize(values):
    center = values - jnp.mean(values, -1, keepdims=True)
    inv_dev = lax.rsqrt(jnp.mean(center * center, -1, keepdims=True) + 1e-05)
    return center * inv_dev, inv_dev


def norm_back(upstream, gain, normed, inv_dev):
    scaled = upstream * gain
    inner = (
        scaled
        - jnp.mean(scaled, -1, keepdims=True)
        - normed * jnp.mean(scaled * normed, -1, keepdims=True)
    )
    return inner * inv_dev


def head_place():
    me = lax.axis_index("head")
    core = lax.rem(me, 2)
    side = me // 2
    return core, side, me + 1 - 2 * core, me + 2 - 4 * side


def greet(peers):
    barrier = pltpu.get_barrier_semaphore()
    for peer in peers:
        pl.semaphore_signal(barrier, inc=1, device_id=peer, device_id_type=MESH)


def await_greetings(count):
    pl.semaphore_wait(pltpu.get_barrier_semaphore(), count)


STEPS = {
    "project": (1, 0, 4, 5),
    "score": (1, 2, 4, 6),
    "weigh": (1, 3, 4, 7),
    "mix": (1, 3, 4, 7),
    "attn_forward": (8, 6, 7, 9),
    "feed": (10, 8, 9, 11),
    "mid_core": (13, 9, 11, 12),
    "mid_chip": (16, 11, 13, 15),
    "back_first": (20, 19, 17, 15),
    "back_second": (20, 19, 17, 16),
    "back_third": (21, 19, 18, 16),
    "in_core": (22, 21, 20, 18),
    "in_chip": (23, 22, 21, 20),
    "out_core": (15, 20, 23, 13),
    "out_chip": (21, 22, 25, 23),
    "merge": (2, 5, 8),
    "cast": (0, 1),
    "clear": 5,
    "wide": (11, 15, 13, 14, 12, 14, 13),
    "pair": (12, 20, 15, 17, 14, 18, 16, 21, 22, 21, 22, 23, 23),
    "rest": (22, 23, 23, 20, 22, 20, 24, 22, 24, 23, 24, 24, 24),
    "update": (24, 25, 25, 25),
    "last_forward": 11,
    "first_backward": 9,
    "all": 26,
}


class Gather:
    def __init__(self, box, sems, axis):
        self.box, self.sems, self.axis = box, sems, axis
        self.count = box.shape[0]
        self.me = lax.axis_index(axis)

    def copy(self, k, slot):
        return pltpu.make_async_remote_copy(
            src_ref=self.box.at[slot],
            dst_ref=self.box.at[slot],
            send_sem=self.sems.at[0, k],
            recv_sem=self.sems.at[1, slot],
            device_id={self.axis: lax.rem(self.me + k, self.count)},
            device_id_type=MESH,
        )

    def each(self, action):
        def step(k, carry):
            action(k)
            return carry

        lax.fori_loop(1, self.count, step, 0)

    def start(self):
        self.each(lambda k: self.copy(k, self.me).start())

    def total(self):
        self.each(lambda k: self.copy(k, lax.rem(self.me + k, self.count)).wait_recv())
        return lax.fori_loop(
            1, self.count, lambda i, running: running + self.box[i], self.box[0]
        )

    def settle(self):
        self.each(lambda k: self.copy(k, self.me).wait_send())


def others(axis, count):
    me = lax.axis_index(axis)
    return [{axis: lax.rem(me + k, count)} for k in range(1, count)]


def pick(lane, values):
    row = jnp.zeros(lane.shape, f32)
    for at, value in enumerate(values):
        row = jnp.where(lane == at, value, row)
    return row


class HeadSum:
    def __init__(self, part, whole, from_core, from_chip, sems, place, home=False, chip_at=0):
        self.part, self.whole, self.home, self.chip_at = part, whole, home, chip_at
        self.from_core, self.from_chip, self.sems = from_core, from_chip, sems
        self.core, self.side, self.sibling, self.across = place

    def copy(self, src, dst, stage, c, peer):
        return pltpu.make_async_remote_copy(
            src_ref=src,
            dst_ref=dst,
            send_sem=self.sems.at[0, stage, c],
            recv_sem=self.sems.at[1, stage, c],
            device_id={"head": peer},
            device_id_type=MESH,
        )

    def pair(self, ref, c):
        return ref.at[pl.ds(2 * c, 2)]

    def mine(self, c):
        return self.whole.at[pl.ds(4 * c + 2 * self.core, 2)]

    def to_core(self, c):
        src = self.part.at[pl.ds(4 * c + 2 * (1 - self.core), 2)]
        return self.copy(src, self.pair(self.from_core, c), 0, c, self.sibling)

    def to_chip(self, c):
        return self.copy(
            self.pair(self.from_core, c),
            self.from_chip.at[pl.ds(self.chip_at + 2 * c, 2)],
            1,
            c,
            self.across,
        )

    def back_core(self, c):
        src = self.pair(self.from_core, c) if self.home else self.mine(c)
        return self.copy(src, self.mine(c), 2, c, self.sibling)

    def keep(self, c):
        return pltpu.make_async_copy(
            self.pair(self.from_core, c), self.mine(c), self.sems.at[0, 3, c]
        )

    def store(self, c, values):
        quarter = self.part.shape[1]
        for i in range(4):
            self.part[4 * c + i] = values[i * quarter : (i + 1) * quarter]

    def start(self, c):
        self.to_core(c).start()

    def reduce_core(self, c):
        self.to_core(c).wait()
        for half in range(2):
            self.from_core[2 * c + half] = (
                self.from_core[2 * c + half] + self.part[4 * c + 2 * self.core + half]
            )
        self.to_chip(c).start()

    def reduce_chip(self, c, finish):
        self.to_chip(c).wait()
        for half in range(2):
            total = self.from_core[2 * c + half] + self.from_chip[self.chip_at + 2 * c + half]
            result = finish(total, c, half)
            if self.home:
                self.from_core[2 * c + half] = result
            else:
                self.whole[4 * c + 2 * self.core + half] = result
        self.back_core(c).start()
        if self.home:
            self.keep(c).start()

    def arrive(self, c):
        self.back_core(c).wait()
        if self.home:
            self.keep(c).wait()


class HeadGather:
    def __init__(self, slot, sems, place):
        self.slot, self.sems = slot, sems
        self.core, self.side, self.sibling, self.across = place
        self.me = 2 * self.side + self.core

    def copy(self, stage, owner, c, peer):
        ref = self.slot(c, owner)
        return pltpu.make_async_remote_copy(
            src_ref=ref,
            dst_ref=ref,
            send_sem=self.sems.at[0, stage, c],
            recv_sem=self.sems.at[1, stage, c],
            device_id={"head": peer},
            device_id_type=MESH,
        )

    def over(self, c):
        return self.copy(0, self.me, c, self.across)

    def beside(self, c):
        return self.copy(1, self.me, c, self.sibling)

    def onward(self, c):
        return self.copy(2, self.across, c, self.sibling)

    def start(self, c):
        self.over(c).start()
        self.beside(c).start()

    def forward(self, c):
        self.over(c).wait_recv()
        self.onward(c).start()

    def arrive(self, c):
        self.over(c).wait_send()
        self.beside(c).wait()
        self.onward(c).wait()


class WeightGather:
    def __init__(self, slot, sems, place):
        self.slot, self.sems = slot, sems
        self.core, self.side, self.sibling, self.across = place
        self.me = 2 * self.side + self.core
        batch = lax.axis_index("batch")
        self.parity = lax.rem(batch, 2)
        self.pair = batch + 1 - 2 * self.parity

    def copy(self, stage, ref, device):
        return pltpu.make_async_remote_copy(
            src_ref=ref,
            dst_ref=ref,
            send_sem=self.sems.at[0, stage, 0],
            recv_sem=self.sems.at[1, stage, 0],
            device_id=device,
            device_id_type=MESH,
        )

    def half(self, owner):
        ref = self.slot(owner)
        columns = ref.shape[2] // 2
        return ref.at[:, :, pl.ds(pl.multiple_of(self.parity * columns, 128), columns)]

    def over(self):
        return self.copy(0, self.half(self.me), {"head": self.across})

    def beside(self):
        return self.copy(1, self.slot(self.me), {"head": self.sibling})

    def onward(self):
        return self.copy(2, self.slot(self.across), {"head": self.sibling})

    def swap(self):
        return self.copy(3, self.half(self.across), {"batch": self.pair})

    def start(self):
        self.over().start()
        self.beside().start()

    def trade(self):
        self.over().wait_recv()
        self.swap().start()

    def forward(self):
        self.swap().wait_recv()
        self.onward().start()

    def arrive(self):
        self.over().wait_send()
        self.swap().wait_send()
        self.beside().wait()
        self.onward().wait()


class BatchScatter:
    def __init__(self, slices, from_pair, from_rest, pair_sems, rest_sems, pieces):
        self.slices, self.from_pair, self.from_rest = slices, from_pair, from_rest
        self.pair_sems, self.rest_sems, self.pieces = pair_sems, rest_sems, pieces
        me = lax.axis_index("batch")
        self.parity, self.place = lax.rem(me, 2), me // 2
        self.pair = me + 1 - 2 * self.parity
        self.count = slices.shape[1]

    def exchange(self, p):
        columns = pl.ds(*self.pieces[p])
        return pltpu.make_async_remote_copy(
            src_ref=self.slices.at[1 - self.parity, :, :, columns],
            dst_ref=self.from_pair.at[:, :, columns],
            send_sem=self.pair_sems.at[0, p],
            recv_sem=self.pair_sems.at[1, p],
            device_id={"batch": self.pair},
            device_id_type=MESH,
        )

    def deliver(self, p, k):
        columns = pl.ds(*self.pieces[p])
        other = lax.rem(self.place + k, self.count)
        return pltpu.make_async_remote_copy(
            src_ref=self.from_pair.at[other, :, columns],
            dst_ref=self.from_rest.at[k - 1, :, columns],
            send_sem=self.rest_sems.at[0, p, k - 1],
            recv_sem=self.rest_sems.at[1, p, k - 1],
            device_id={"batch": other * 2 + self.parity},
            device_id_type=MESH,
        )

    def each(self, p, action):
        def step(k, carry):
            action(self.deliver(p, k))
            return carry

        lax.fori_loop(1, self.count, step, 0)

    def start(self):
        for p in range(len(self.pieces)):
            self.exchange(p).start()

    def reduce_pair(self, p):
        self.exchange(p).wait_recv()
        columns = pl.ds(*self.pieces[p])

        def step(i, carry):
            self.from_pair[i, :, columns] = (
                self.from_pair[i, :, columns] + self.slices[self.parity, i, :, columns]
            )
            return carry

        lax.fori_loop(0, self.count, step, 0)
        self.each(p, lambda copy: copy.start())

    def reduce_rest(self, out, p):
        self.each(p, lambda copy: copy.wait_recv())
        columns = pl.ds(*self.pieces[p])
        out[:, columns] = self.from_pair[self.place, :, columns]

        def step(k, carry):
            out[:, columns] += self.from_rest[k - 1, :, columns]
            return carry

        lax.fori_loop(1, self.count, step, 0)

    def settle(self):
        for p in range(len(self.pieces)):
            self.exchange(p).wait_send()
            self.each(p, lambda copy: copy.wait_send())


def add_slices(ref, half, values):
    count, share = ref.shape[1], ref.shape[2]
    for i in range(count):
        owner = half * count + i
        ref[owner % 2, owner // 2] += values[i * share : (i + 1) * share]


def layer_kernel(
    length_ref,
    gains_ref,
    moment_ref,
    heads_rows,
    heads_cols,
    merge_rows,
    merge_cols,
    expand_rows,
    expand_cols,
    shrink_rows,
    shrink_cols,
    residual_ref,
    cotangent_ref,
    heads_ref,
    merge_ref,
    expand_ref,
    shrink_ref,
    out_ref,
    in_grad_ref,
    heads_own,
    merge_own,
    expand_own,
    shrink_own,
    side_scale,
    lane_scale,
    side_next,
    lane_next,
    gains_grad,
    moment_next,
    gains_next,
    rms_ref,
    gain_one,
    gain_two,
    weight_squares,
    lane_old,
    lane_sum,
    share_sum,
    flat,
    lane_box,
    side_box,
    share_box,
    square_box,
    square_share,
    heads_low,
    merge_low,
    expand_low,
    shrink_low,
    first_ref,
    q_ref,
    k_ref,
    v_ref,
    qt_ref,
    kt_ref,
    vt_ref,
    mixed_ref,
    att_ref,
    logsum_ref,
    middle,
    part,
    mlp_part,
    from_core,
    from_chip,
    mid_chip,
    mlp_sums,
    middle_own,
    second,
    out_low,
    active,
    expand_back,
    second_cols,
    out_cols,
    attended_cols,
    mid_low,
    back_rows,
    back_cols,
    joint_back,
    queries,
    grad_cols,
    query_rows,
    grad_rows,
    row_stats,
    scores,
    probs_low,
    score_low,
    key_sum,
    value_sum,
    query_sum,
    heads_slices,
    merge_slices,
    expand_slices,
    shrink_slices,
    heads_pair,
    heads_rest,
    merge_pair,
    merge_rest,
    expand_pair,
    expand_rest,
    shrink_pair,
    shrink_rest,
    load_sems,
    sum_sems,
    pair_sems,
    rest_sems,
    lane_sems,
    side_sems,
    share_sems,
    square_sems,
    square_share_sems,
):
    chunks, rows, width = first_ref.shape
    quarter = rows // 4
    local = q_ref.shape[2]
    heads = local // HEAD_DIM
    last = chunks - 1
    place = head_place()
    core = place[0]
    me = 2 * place[1] + core

    def merge_slot(owner):
        count = merge_ref.shape[0]
        return middle.at[pl.ds(4 + count * owner, count)]

    merge_gather = WeightGather(merge_slot, sum_sems.at[4], place)
    mixed_gather = HeadGather(
        lambda c, owner: mixed_ref.at[4 * c + owner], sum_sems.at[0], place
    )
    mid_sum = HeadSum(part, middle, from_core, mid_chip, sum_sems.at[1], place)
    in_sum = HeadSum(part, in_grad_ref, from_core, from_chip, sum_sems.at[2], place, True)
    out_sum = HeadSum(
        mlp_part, out_ref, mlp_sums, mlp_sums, sum_sems.at[3], place, True, 2 * chunks
    )
    third = expand_slices.shape[3] // 3
    shrink_pieces = tuple((i * third, third) for i in range(3))
    expand_pieces = shrink_pieces[:2] + tuple((2 * third + i * third // 2, third // 2) for i in range(2))
    heads_pieces = tuple((at, min(128, 3 * local - at)) for at in range(0, 3 * local, 128))
    scatters = [
        BatchScatter(s, p, r, pair_sems.at[i], rest_sems.at[i], pieces)
        for i, (s, p, r, pieces) in enumerate(
            (
                (shrink_slices, shrink_pair, shrink_rest, shrink_pieces),
                (expand_slices, expand_pair, expand_rest, expand_pieces),
                (merge_slices, merge_pair, merge_rest, ((0, local),)),
                (heads_slices, heads_pair, heads_rest, heads_pieces),
            )
        )
    ]
    shrink_scatter, expand_scatter, merge_scatter, heads_scatter = scatters

    def load(src, dst, i):
        return pltpu.make_async_copy(src, dst, load_sems.at[i])

    def load_rows(c):
        return load(residual_ref.at[pl.ds(4 * c, 4)], part.at[pl.ds(4 * c, 4)], c)

    def load_cotangent(c):
        return load(
            cotangent_ref.at[pl.ds(4 * c, 4)], mlp_part.at[pl.ds(4 * c, 4)], chunks + c
        )

    def load_own(c):
        src = residual_ref.at[pl.ds(4 * c + 2 * core, 2)]
        return load(src, mid_chip.at[pl.ds(2 * c, 2)], 2 * chunks + c)

    run = 2 * chunks - 2

    def load_weight(src, i):
        count = src.shape[0]
        spans = ((0, 2, run), (run, 2 * chunks + 2, count - run))
        return [
            load(src.at[pl.ds(at, n)], mlp_sums.at[pl.ds(to, n)], 3 * chunks + 2 * i + half)
            for half, (at, to, n) in enumerate(spans)
        ]

    load_heads, load_expand, load_shrink = (
        load_weight(src, i) for i, src in enumerate((heads_ref, expand_ref, shrink_ref))
    )
    load_merge = load(merge_ref, merge_slot(me), 3 * chunks + 6)

    def start_all(copies):
        for copy in copies:
            copy.start()

    def wait_all(copies):
        for copy in copies:
            copy.wait()

    def each_chunk(action):
        def step(c, carry):
            action(c)
            return carry

        lax.fori_loop(0, chunks, step, 0)

    load_merge.start()
    start_all(load_heads)

    def open_loads(c):
        load_rows(c).start()
        load_cotangent(c).start()

    each_chunk(open_loads)
    share = heads_own.shape[0]
    deep = active.shape[0] > rows
    batch_count, head_count = lane_box.shape[0], side_box.shape[0]
    peers = others("batch", batch_count) + others("head", head_count)
    greet(peers)

    def cast_blocks(count, low, which):
        weight_squares[which] = jnp.zeros(weight_squares.shape[1:], f32)

        def step(i, carry):
            block = mlp_sums[2 + i + 2 * (i // run)]
            low[band(i * quarter, quarter), :] = block.astype(bf16)
            weight_squares[which] += fold(block * block, jnp.sum)
            return carry

        lax.fori_loop(0, count, step, 0)

    wait_all(load_heads)
    cast_blocks(heads_ref.shape[0], heads_low, 0)
    start_all(load_expand)
    load_merge.wait()
    await_greetings(len(peers))
    merge_gather.start()
    length = length_ref[0]
    gain_in, gain_mid = gains_ref[0:1, :], gains_ref[1:2, :]
    eye_local, eye_rows = identity(local), identity(rows)
    head_row = lax.broadcasted_iota(jnp.int32, (local, 1), 0) // HEAD_DIM
    head_col = lax.broadcasted_iota(jnp.int32, (1, local), 1) // HEAD_DIM
    key_row = lax.broadcasted_iota(jnp.int32, (rows, 1), 0)
    gain_one[...] = jnp.zeros_like(gain_one)
    gain_two[...] = jnp.zeros_like(gain_two)

    def live_rows(at, count):
        return (at + lax.broadcasted_iota(jnp.int32, (count, 1), 0) < length).astype(f32)

    def project(c):
        load_rows(c).wait()

        def norm_tile(at):
            values = part[4 * c + at // quarter, band(lax.rem(at, quarter), 64), :]
            first_ref[c, band(at, 64), :] = (normalize(values)[0] * gain_in).astype(bf16)

        tiles(rows, 64, norm_tile)
        normed = first_ref[c]
        live = live_rows(c * rows, rows)
        for which, (row_ref, col_ref) in enumerate(((q_ref, qt_ref), (k_ref, kt_ref), (v_ref, vt_ref))):
            joint = mm_nt(normed, heads_low[which * local : (which + 1) * local, :]).astype(bf16)
            scale = HEAD_DIM ** (-0.5) if which == 0 else live
            joint = (joint.astype(f32) * scale).astype(bf16)
            row_ref[c] = joint
            col_ref[c] = mm_nt(eye_local, joint).astype(bf16)

    def limit_of(c):
        return jnp.minimum(
            c * rows + lax.broadcasted_iota(jnp.int32, (1, rows), 1), length - 1
        )

    def attend_score(c):
        for h in range(heads):
            queries[h] = jnp.where(head_row == h, qt_ref[c].astype(f32), 0.0).astype(bf16)

        def score(kb, tops, limit=None):
            fresh = []
            for h in range(heads):
                s = mm(k_ref[kb], queries[h])
                scores[h, band(kb * rows, rows), :] = s
                square = s * s
                if limit is not None:
                    square = jnp.where(key_row + kb * rows <= limit, square, 0.0)
                fresh.append(jnp.maximum(tops[h], fold(square, jnp.max)))
            return tuple(fresh)

        tops = lax.fori_loop(0, c, score, (jnp.zeros((8, rows), f32),) * heads)
        tops = score(c, tops, limit_of(c))
        for h in range(heads):
            top = jnp.max(tops[h], 0, keepdims=True)
            row_stats[0, h : h + 1, :] = jnp.sqrt(top + 1.0) * LOG2E

    def attend_weigh(c):
        tile = 32
        limit = limit_of(c)
        for h in range(heads):
            row_stats[1, h : h + 1, :] = jnp.zeros((1, rows), f32)

        def weigh(at, norms, limit):
            keep = key_row[:tile] + at <= limit
            fresh = []
            for h in range(heads):
                s = scores[h, band(at, tile), :]
                square = s * s + 1.0
                power = square * lax.rsqrt(square) * LOG2E - row_stats[0, h : h + 1, :]
                weight = jnp.exp2(jnp.where(keep, power, -1e30))
                scores[h, band(at, tile), :] = jnp.tanh(s) * weight
                fresh.append(norms[h] + fold(weight, jnp.sum))
            return tuple(fresh)

        def four(i, norms):
            for j in range(4):
                norms = weigh((4 * i + j) * tile, norms, limit)
            return norms

        norms = lax.fori_loop(
            0, (c + 1) * (rows // (4 * tile)), four, (jnp.zeros((8, rows), f32),) * heads
        )
        for h in range(heads):
            norm = jnp.sum(norms[h], 0, keepdims=True)
            row_stats[1, h : h + 1, :] = 1.0 / norm
            logsum_ref[c, h : h + 1, :] = row_stats[0, h : h + 1, :] + jnp.log(norm) * LOG2E

    def attend_mix(c):
        mixed_ref[4 * c + me] = jnp.zeros(mixed_ref.shape[1:], f32)

        def mix(kb, carry):
            for h in range(heads):
                mine = slice(h * HEAD_DIM, (h + 1) * HEAD_DIM)
                probs = scores[h, band(kb * rows, rows), :] * row_stats[1, h : h + 1, :]
                mixed_ref[4 * c + me, mine, :] += mm(vt_ref[kb, mine, :], probs.astype(bf16))
            return carry

        lax.fori_loop(0, c + 1, mix, 0)

    def attend_end(c):
        mixed_gather.start(c)
        own = mixed_ref[4 * c + me].astype(bf16)
        att_ref[c] = mm_nt(eye_rows, own).astype(bf16)

    def cast_merge():
        merge_gather.arrive()
        weight_squares[1] = jnp.zeros(weight_squares.shape[1:], f32)
        for owner in range(4):

            def cast(i, carry):
                block = middle[4 + merge_ref.shape[0] * owner + i]
                merge_low[band(owner * local + i * quarter, quarter), :] = block.astype(bf16)

                @pl.when(owner == me)
                def _():
                    weight_squares[1] += fold(block * block, jnp.sum)

                return carry

            lax.fori_loop(0, merge_ref.shape[0], cast, 0)

    def add_attended(c):
        mixed_gather.arrive(c)
        for owner in range(4):
            attended_cols[owner * local : (owner + 1) * local, :] = mixed_ref[
                4 * c + owner
            ].astype(bf16)
        out = mm_tn(attended_cols[...], merge_low[...])
        for i in range(4):
            rows_in = slice(i * quarter, (i + 1) * quarter)
            middle[4 * c + i] = part[4 * c + i] + out[rows_in]
        for half in range(2):
            middle_own[2 * c + half] = middle[4 * c + 2 * core + half]

    def feed(c):
        base = c * rows if deep else 0
        add_attended(c)
        load_cotangent(c).wait()

        def norm_tile(at):
            block, inside = 4 * c + at // quarter, band(lax.rem(at, quarter), 64)
            second[band(at, 64), :] = (normalize(middle[block, inside, :])[0] * gain_mid).astype(bf16)
            grad = mlp_part[block, inside, :] * live_rows(c * rows + at, 64)
            out_low[band(at, 64), :] = grad.astype(bf16)

        tiles(rows, 64, norm_tile)
        for half in range(2):
            block = 4 * c + 2 * core + half
            at = c * rows + (2 * core + half) * quarter
            middle[block] = mlp_part[block] * live_rows(at, quarter)
        mid_sum.store(c, mm(second[...], expand_low[...]))
        out_sum.store(c, mm_nt(out_low[...], shrink_low[...]))

        def gelu_tile(at):
            block, inside = 4 * c + at // quarter, band(lax.rem(at, quarter), 32)
            value = part[block, inside, :]
            square = value * value
            bend = jnp.tanh(GELU_A * value * (1.0 + GELU_B * square))
            half = 0.5 * (1.0 + bend)
            active[band(base + at, 32), :] = (value * half).astype(bf16)
            slope = half + 0.5 * value * (1.0 - bend * bend) * (
                GELU_A + (3.0 * GELU_A * GELU_B) * square
            )
            expand_back[band(base + at, 32), :] = (slope * mlp_part[block, inside, :]).astype(bf16)

        tiles(rows, 32, gelu_tile)
        here = band(base, rows)
        mid_sum.store(c, mm_nt(expand_back[here, :], expand_low[...]))
        mid_sum.start(c)
        out_sum.store(c, mm(active[here, :], shrink_low[...]))
        out_sum.start(c)
        if deep:
            lanes_here = band(c * rows, rows)
            second_cols[:, lanes_here] = second[...].T
            out_cols[:, lanes_here] = out_low[...].T
        else:
            for half in range(2):
                columns = slice(half * (width // 2), (half + 1) * (width // 2))
                add_slices(shrink_slices, half, mm_tn(out_low[:, columns], active[...]))
                add_slices(expand_slices, half, mm_tn(second[:, columns], expand_back[...]))

    def send_wide(scatter, p):
        if deep:
            left, right = (
                (out_cols, active) if scatter is shrink_scatter else (second_cols, expand_back)
            )
            at, size = scatter.pieces[p]
            columns = slice(at, at + size)
            for half in range(2):
                side = left[half * (width // 2) : (half + 1) * (width // 2), :]
                values = mm(side, right[:, columns])
                for i in range(scatter.count):
                    owner = half * scatter.count + i
                    scatter.slices[owner % 2, owner // 2, :, columns] = values[
                        i * share : (i + 1) * share
                    ]
        scatter.exchange(p).start()

    def finish_mid(values, c, half):
        normed, inv_dev = normalize(middle_own[2 * c + half])
        gain_two[...] += fold(values * normed, jnp.sum)
        upstream = middle[4 * c + 2 * core + half]
        return upstream + norm_back(values, gain_mid, normed, inv_dev)

    def finish_out(values, c, half):
        return middle_own[2 * c + half] + values

    def finish_in(values, c, half):
        normed, inv_dev = normalize(mid_chip[2 * c + half])
        gain_one[...] += fold(values * normed, jnp.sum)
        grad = middle[4 * c + 2 * core + half]
        return grad + norm_back(values, gain_in, normed, inv_dev)

    def attend_back_open(c):
        mid_sum.arrive(c)

        def low_tile(at):
            block, inside = 4 * c + at // quarter, band(lax.rem(at, quarter), 64)
            mid_low[band(at, 64), :] = middle[block, inside, :].astype(bf16)

        tiles(rows, 64, low_tile)
        merge_own_low = merge_low[band(me * local, local), :]
        back_rows[...] = mm_nt(mid_low[...], merge_own_low).astype(bf16)
        back_cols[...] = mm_nt(merge_own_low, mid_low[...]).astype(bf16)
        for half in range(2):
            columns = slice(half * (width // 2), (half + 1) * (width // 2))
            add_slices(merge_slices, half, mm_tn(mid_low[:, columns], att_ref[c]))

        for h in range(heads):
            queries[h] = jnp.where(head_row == h, qt_ref[c].astype(f32), 0.0).astype(bf16)
            columns = jnp.where(head_row == h, back_cols[...].astype(f32), 0.0)
            row_stats[2, h : h + 1, :] = jnp.sum(columns * mixed_ref[4 * c + me], 0, keepdims=True)
            grad_cols[h] = columns.astype(bf16)
            stack = slice(h * rows, (h + 1) * rows)
            query_rows[stack, :] = jnp.where(head_col == h, q_ref[c].astype(f32), 0.0).astype(bf16)
            grad_rows[stack, :] = jnp.where(head_col == h, back_rows[...].astype(f32), 0.0).astype(bf16)
        query_sum[...] = jnp.zeros_like(query_sum)

    def back_block(c, kb, diagonal):
        tile = 32
        limit = limit_of(c)
        for h in range(heads):
            scores[h, :rows, :] = mm(k_ref[kb], queries[h])
            scores[h, rows : 2 * rows, :] = mm(v_ref[kb], grad_cols[h])
        for h in range(heads):
            for i in range(rows // tile):
                at = slice(i * tile, (i + 1) * tile)
                skip = rows // 2 if diagonal and i * tile >= rows // 2 else 0
                s = scores[h, at, skip:]
                grad = scores[h, rows + i * tile : rows + (i + 1) * tile, skip:]
                square = s * s + 1.0
                inverse = lax.rsqrt(square)
                power = square * inverse * LOG2E - logsum_ref[c, h : h + 1, skip:]
                if diagonal:
                    keep = key_row[:tile] + (kb * rows + i * tile) <= limit[:, skip:]
                    power = jnp.where(keep, power, -1e30)
                weight = jnp.exp2(power)
                bend = jnp.tanh(s)
                slope = s * inverse
                pull = bend * grad
                change = grad + pull * (slope - bend) - slope * row_stats[2, h : h + 1, skip:]
                lanes = slice(h * rows + skip, (h + 1) * rows)
                probs_low[at, lanes] = (bend * weight).astype(bf16)
                score_low[at, lanes] = (weight * change).astype(bf16)
                if skip:
                    empty = slice(h * rows, h * rows + skip)
                    probs_low[at, empty] = jnp.zeros((tile, skip), bf16)
                    score_low[at, empty] = jnp.zeros((tile, skip), bf16)
        value_sum[kb] += mm(probs_low[...], grad_rows[...])
        key_sum[kb] += mm(score_low[...], query_rows[...])
        for h in range(heads):
            mine = slice(h * HEAD_DIM, (h + 1) * HEAD_DIM)
            query_sum[mine, :] += mm(kt_ref[kb, mine, :], score_low[:, h * rows : (h + 1) * rows])

    def attend_back(c, j):
        low, high = (c + 1) * j // 3, (c + 1) * (j + 1) // 3

        def one(kb, carry):
            back_block(c, kb, False)
            return carry

        lax.fori_loop(low, jnp.minimum(high, c), one, 0)

        @pl.when(j == 2)
        def _():
            back_block(c, c, True)

    def attend_back_end(c):
        query_low = (query_sum[...] * HEAD_DIM ** (-0.5)).astype(bf16)
        joint_back[:, :local] = mm_nt(eye_rows, query_low).astype(bf16)
        joint_back[:, local : 2 * local] = key_sum[c].astype(bf16)
        joint_back[:, 2 * local :] = value_sum[c].astype(bf16)
        in_sum.store(c, mm(joint_back[...], heads_low[...]))
        in_sum.start(c)
        for half in range(2):
            columns = slice(half * (width // 2), (half + 1) * (width // 2))
            add_slices(heads_slices, half, mm_tn(first_ref[c, :, columns], joint_back[...]))

    lanes = Gather(lane_box, lane_sems, "batch")
    sides = Gather(side_box, side_sems, "head")
    shares = Gather(share_box, share_sems, "head")
    squares = Gather(square_box, square_sems, "batch")
    square_shares = Gather(square_share, square_share_sems, "head")
    grads = (heads_own, merge_own, expand_own, shrink_own)
    row_lens = (width, width, width, head_count * shrink_own.shape[1])
    col_lens = (
        head_count * heads_own.shape[1],
        width,
        head_count * expand_own.shape[1],
        width,
    )
    on_side = (True, False, True, False)
    decay = 1.0 - STEP ** (-0.8)
    lane = lax.broadcasted_iota(jnp.int32, (1, width), 1)
    narrow = lax.broadcasted_iota(jnp.int32, (share, 128), 1)

    def whole_sum(values):
        return jnp.sum(jnp.sum(values, 0, keepdims=True), 1, keepdims=True)

    def clear():
        late = (heads_slices, merge_slices)
        for ref in late if deep else (expand_slices, shrink_slices, *late):

            def zero(i, carry):
                for parity in range(2):
                    ref[parity, i] = jnp.zeros(ref.shape[2:], f32)
                return carry

            lax.fori_loop(0, ref.shape[1], zero, 0)
        key_sum[...] = jnp.zeros_like(key_sum)
        value_sum[...] = jnp.zeros_like(value_sum)
        flat[...] = jnp.zeros_like(flat)
        for i, ref in enumerate((heads_rows, merge_cols, expand_rows, shrink_cols)):
            flat[i, :share] = ref[...]
        flat[...] = flat[...].T
        lane_old[...] = jnp.zeros_like(lane_old)
        for i in range(3):
            lane_old[0:1, i * local : (i + 1) * local] = heads_cols[i : i + 1, :]
        for i, ref in enumerate((merge_rows, expand_cols, shrink_rows)):
            lane_old[i + 1, : ref.shape[0]] = ref[...]
        lane_box[lanes.me] = jnp.zeros(lane_box.shape[1:], f32)
        side_box[sides.me] = jnp.zeros(side_box.shape[1:], f32)

    def statistics(i):
        square = grads[i][...] * grads[i][...]
        side_sum = jnp.sum(square, 1, keepdims=True)
        side_box[sides.me] = jnp.where(narrow == i, side_sum, side_box[sides.me])
        lane_box[lanes.me, i : i + 1, : square.shape[1]] = jnp.sum(square, 0, keepdims=True)

    def open_update():
        statistics(0)
        mine = lanes.me
        lane_box[mine, 4:5, :] = 0.5 * jnp.sum(gain_one[...], 0, keepdims=True)
        lane_box[mine, 5:6, :] = 0.5 * jnp.sum(gain_two[...], 0, keepdims=True)
        old = jnp.sum(flat[:share], 0, keepdims=True)
        lane_box[mine, 6:7, :] = pick(
            lane,
            [whole_sum(weight_squares[i]) / batch_count for i in range(4)]
            + [old[:, 0:1], old[:, 2:3]],
        )
        lanes.start()
        sides.start()

    def factors():
        total = lanes.total()
        lane_sum[...] = total
        mine = shares.me
        share_box[mine, 0:2, :] = total[4:6]
        share_box[mine, 2:3, :] = total[6:7] + pick(
            lane - 6,
            [jnp.sum(total[i : i + 1], 1, keepdims=True) for i in range(4)]
            + [jnp.sum(lane_old[i : i + 1, :], 1, keepdims=True) for i in (1, 3)],
        )
        share_box[mine, 3:8, :] = jnp.zeros((5, width), f32)
        shares.start()
        side_sum = sides.total()
        local_squares, side_factors, sides_new = [], [], []
        lane_next[...] = jnp.zeros_like(lane_next)
        lane_scale[...] = jnp.zeros_like(lane_scale)
        for i, grad in enumerate(grads):
            columns = grad.shape[1]
            side_len, lane_len = (
                (col_lens[i], row_lens[i]) if on_side[i] else (row_lens[i], col_lens[i])
            )
            side = decay * flat[:share, i : i + 1] + (1.0 - decay) * (
                side_sum[:, i : i + 1] / side_len + tiny_term
            )
            across = decay * lane_old[i : i + 1, :columns] + (1.0 - decay) * (
                lane_sum[i : i + 1, :columns] / lane_len + tiny_term
            )
            sides_new.append(side)
            lane_next[i : i + 1, :columns] = across
            side_factors.append(lax.rsqrt(side))
            lane_factor = lax.rsqrt(across)
            lane_scale[i : i + 1, :columns] = lane_factor
            update = grad[...] * side_factors[i] * lane_factor
            local_squares.append(whole_sum(update * update))
        side_next[...] = pick(narrow, sides_new)
        side_scale[...] = pick(narrow, side_factors)
        square_box[squares.me] = pick(
            lax.broadcasted_iota(jnp.int32, (8, 128), 1), local_squares
        )
        squares.start()

    def share_squares():
        share_sum[...] = shares.total()
        gain_grad = share_sum[0:2, :]
        gains_grad[...] = gain_grad
        moment_next[...] = decay * moment_ref[...] + (1.0 - decay) * (
            gain_grad * gain_grad + tiny_term
        )
        square_share[square_shares.me] = squares.total()
        square_shares.start()

    def close_update():
        scalar = [share_sum[2:3, i : i + 1] for i in range(12)]
        old_totals = (scalar[4] / head_count, scalar[10], scalar[5] / head_count, scalar[11])
        means = [
            decay * old_totals[i] / row_lens[i]
            + (1.0 - decay) * (scalar[6 + i] / (row_lens[i] * col_lens[i]) + tiny_term)
            for i in range(4)
        ]
        gain_step = gains_grad[...] * lax.rsqrt(moment_next[...])
        total = whole_sum(gain_step * gain_step)
        matrix_squares = square_shares.total()
        for i in range(4):
            total = total + means[i] * matrix_squares[0:1, i : i + 1]
        count = 4.0 * width * width + 2.0 * width * row_lens[3] + 2.0 * width
        rms = jnp.sqrt(total / count)
        rms_ref[...] = jnp.broadcast_to(rms, (8, 128))
        clip = 1.0 / jnp.maximum(1.0, rms / clip_level)
        side_scale[...] = side_scale[...] * pick(
            narrow[:1],
            [
                jnp.sqrt(means[i])
                * jnp.sqrt(scalar[i] / (1.0 * row_lens[i] * col_lens[i]))
                * clip
                for i in range(4)
            ],
        )
        gains = gains_ref[...]
        gains_next[...] = (
            gains - jnp.sqrt(jnp.mean(gains * gains, 1, keepdims=True)) * clip * gain_step
        )


    pieces = [(shrink_scatter, p, shrink_own) for p in range(len(shrink_pieces))]
    pieces += [(expand_scatter, p, expand_own) for p in range(len(expand_pieces))]
    pieces += [(merge_scatter, 0, merge_own)]
    pieces += [(heads_scatter, p, heads_own) for p in range(len(heads_pieces))]

    def step(u, carry):
        def at_chunk(name, action):
            at = STEPS[name]
            c = sum(jnp.where(u == at[i], i, 0) for i in range(1, 4))

            @pl.when((u == at[0]) | (u == at[1]) | (u == at[2]) | (u == at[3]))
            def _():
                action(c)

        def at_step(at, action):
            @pl.when(u == at)
            def _():
                action()

        def mix_and_send(c):
            attend_mix(c)
            attend_end(c)

        def cast_expand():
            wait_all(load_expand)
            cast_blocks(expand_ref.shape[0], expand_low, 2)
            start_all(load_shrink)

        def cast_shrink():
            wait_all(load_shrink)
            cast_blocks(shrink_ref.shape[0], shrink_low, 3)

        def back_first(c):
            attend_back_open(c)

            @pl.when(c == 0)
            def _():
                merge_scatter.start()

            attend_back(c, 0)

        def back_third(c):
            attend_back(c, 2)
            attend_back_end(c)

            @pl.when(c == 0)
            def _():
                heads_scatter.start()

        def finish_chunk(c):
            mid_sum.reduce_chip(c, finish_mid)
            load_own(c).start()

        def finish_inner(c):
            load_own(c).wait()
            in_sum.reduce_chip(c, finish_in)

        @pl.when(u <= STEPS["last_forward"])
        def _():
            at_chunk("project", project)
            at_chunk("score", attend_score)
            at_chunk("weigh", attend_weigh)
            at_chunk("mix", mix_and_send)
            at_chunk("attn_forward", mixed_gather.forward)
            at_step(STEPS["merge"][0], merge_gather.trade)
            at_step(STEPS["merge"][1], merge_gather.forward)
            at_step(STEPS["merge"][2], cast_merge)
            at_step(STEPS["cast"][0], cast_expand)
            at_step(STEPS["cast"][1], cast_shrink)
            at_step(STEPS["clear"], clear)
            at_chunk("feed", feed)

        @pl.when(u >= STEPS["first_backward"])
        def _():
            for i, (scatter, p, _) in enumerate(pieces[: len(STEPS["wide"])]):
                at_step(STEPS["wide"][i], partial(send_wide, scatter, p))
            at_chunk("mid_core", mid_sum.reduce_core)
            at_chunk("mid_chip", finish_chunk)
            at_chunk("back_first", back_first)
            at_chunk("back_second", lambda c: attend_back(c, 1))
            at_chunk("back_third", back_third)
            at_chunk("in_core", in_sum.reduce_core)
            for i, (scatter, p, out) in enumerate(pieces):
                at_step(STEPS["pair"][i], partial(scatter.reduce_pair, p))
            for i, (scatter, p, out) in enumerate(pieces):
                at_step(STEPS["rest"][i], partial(scatter.reduce_rest, out, p))
            for i, out in ((3, shrink_own), (2, expand_own), (1, merge_own)):
                ends = [at for at, piece in zip(STEPS["rest"], pieces) if piece[2] is out]
                at_step(max(ends), partial(statistics, i))
            at_chunk("out_core", out_sum.reduce_core)
            at_chunk("out_chip", lambda c: out_sum.reduce_chip(c, finish_out))
            at_chunk("in_chip", finish_inner)
            for at, action in zip(
                STEPS["update"], (open_update, factors, share_squares, close_update)
            ):
                at_step(at, action)
        return carry

    lax.fori_loop(0, STEPS["all"], step, 0)
    for scatter in scatters:
        scatter.settle()
    for gather in (lanes, sides, shares, squares, square_shares):
        gather.settle()
    each_chunk(out_sum.arrive)
    each_chunk(in_sum.arrive)


def run_layer(lengths, small, residual, cotangent, weights, batch_count, head_count):
    seq_len, width = residual.shape
    rows = CHUNK
    chunks, quarter = seq_len // rows, rows // 4
    local, wide = weights[1].shape[0], weights[3].shape[0]
    heads = local // HEAD_DIM
    count, share = batch_count // 2, width // batch_count
    deep = share % 8 == 0
    tokens = seq_len if deep else rows
    blocks = [m.reshape(-1, quarter, width) for m in (residual, cotangent, *weights)]
    whole = ((4 * chunks, quarter, width), f32)
    pair = ((2 * chunks, quarter, width), f32)
    row_low, col_low = ((chunks, rows, local), bf16), ((chunks, local, rows), bf16)
    low = ((rows, width), bf16)

    def scatter(columns):
        return [((count, share, columns), f32), ((max(count - 1, 1), share, columns), f32)]

    def slices(columns):
        return ((2, count, share, columns), f32)

    vm, hbm = pl.BlockSpec(memory_space=pltpu.VMEM), pl.BlockSpec(memory_space=pl.ANY)
    outs = [
        whole,
        whole,
        ((share, 3 * local), f32),
        ((share, local), f32),
        ((share, wide), f32),
        ((share, wide), f32),
        ((share, 128), f32),
        ((8, width), f32),
        ((share, 128), f32),
        ((8, width), f32),
        ((2, width), f32),
        ((2, width), f32),
        ((2, width), f32),
        ((8, 128), f32),
    ]
    scratch = [
        ((8, width), f32),
        ((8, width), f32),
        ((4, 8, width), f32),
        ((8, width), f32),
        ((8, width), f32),
        ((8, width), f32),
        ((128, 128), f32),
        ((batch_count, 8, width), f32),
        ((head_count, share, 128), f32),
        ((head_count, 8, width), f32),
        ((batch_count, 8, 128), f32),
        ((head_count, 8, 128), f32),
        ((3 * local, width), bf16),
        ((head_count * local, width), bf16),
        ((width, wide), bf16),
        ((wide, width), bf16),
        ((chunks, rows, width), bf16),
        row_low,
        row_low,
        row_low,
        col_low,
        col_low,
        col_low,
        ((head_count * chunks, local, rows), f32),
        row_low,
        ((chunks, 8, rows), f32),
        whole,
        whole,
        whole,
        *[pair] * 3,
        whole,
        pair,
        low,
        low,
        ((tokens, wide), bf16),
        ((tokens, wide), bf16),
        ((width, seq_len) if deep else (16, 128), bf16),
        ((width, seq_len) if deep else (16, 128), bf16),
        ((head_count * local, rows), bf16),
        low,
        ((rows, local), bf16),
        ((local, rows), bf16),
        ((rows, 3 * local), bf16),
        ((heads, local, rows), bf16),
        ((heads, local, rows), bf16),
        ((heads * rows, local), bf16),
        ((heads * rows, local), bf16),
        ((3, 8, rows), f32),
        ((heads, seq_len, rows), f32),
        ((rows, heads * rows), bf16),
        ((rows, heads * rows), bf16),
        ((chunks, rows, local), f32),
        ((chunks, rows, local), f32),
        ((local, rows), f32),
        slices(3 * local),
        slices(local),
        slices(wide),
        slices(wide),
        *scatter(3 * local),
        *scatter(local),
        *scatter(wide),
        *scatter(wide),
        pltpu.SemaphoreType.DMA((3 * chunks + 7,)),
        pltpu.SemaphoreType.DMA((5, 2, 4, chunks)),
        pltpu.SemaphoreType.DMA((4, 2, 5)),
        pltpu.SemaphoreType.DMA((4, 2, 5, max(count - 1, 1))),
        pltpu.SemaphoreType.DMA((2, batch_count)),
        pltpu.SemaphoreType.DMA((2, head_count)),
        pltpu.SemaphoreType.DMA((2, head_count)),
        pltpu.SemaphoreType.DMA((2, batch_count)),
        pltpu.SemaphoreType.DMA((2, head_count)),
    ]
    return pl.pallas_call(
        layer_kernel,
        out_shape=tuple(jax.ShapeDtypeStruct(*o) for o in outs),
        in_specs=[pl.BlockSpec(memory_space=pltpu.SMEM)] + [vm] * len(small) + [hbm] * 6,
        out_specs=(hbm, hbm) + (vm,) * 12,
        scratch_shapes=[pltpu.VMEM(*s) if isinstance(s, tuple) else s for s in scratch],
        compiler_params=pltpu.CompilerParams(
            collective_id=0, has_side_effects=True, vmem_limit_bytes=VMEM_LIMIT
        ),
        name="layer",
    )(lengths, *small, *blocks)


def apply_kernel(
    block_out,
    residual_grad,
    heads_weight,
    merge_weight,
    expand_weight,
    shrink_weight,
    heads_own,
    merge_own,
    expand_own,
    shrink_own,
    side_scale,
    lane_scale,
    side_new,
    lane_new,
    gains_grad,
    moment_new,
    gains_new,
    rms_new,
    block_out_ref,
    residual_grad_ref,
    heads_grad_ref,
    heads_rows_ref,
    heads_cols_ref,
    heads_next_ref,
    merge_grad_ref,
    merge_rows_ref,
    merge_cols_ref,
    merge_next_ref,
    expand_grad_ref,
    expand_rows_ref,
    expand_cols_ref,
    expand_next_ref,
    shrink_grad_ref,
    shrink_rows_ref,
    shrink_cols_ref,
    shrink_next_ref,
    gains_grad_ref,
    gain_moment_ref,
    gains_next_ref,
    rms_ref,
    window,
    master,
    rows_master,
    square,
    staged,
    sems,
):
    width = gains_grad.shape[1]
    share, local, wide = merge_own.shape[0], merge_own.shape[1], shrink_own.shape[1]
    me = lax.axis_index("batch")
    first = pl.multiple_of(jnp.minimum(me * share // 128 * 128, width - 256), 128)
    offset = me * share - first
    heads_at, merge_at = wide, wide + 3 * local
    copies = [
        pltpu.make_async_copy(shrink_weight.at[:, pl.ds(first, 256)], window.at[:wide], sems.at[0]),
        pltpu.make_async_copy(
            heads_weight.at[:, pl.ds(first, 256)], window.at[heads_at:merge_at], sems.at[1]
        ),
        pltpu.make_async_copy(
            merge_weight.at[:, pl.ds(first, 256)], window.at[merge_at:], sems.at[2]
        ),
        pltpu.make_async_copy(expand_weight.at[me], rows_master, sems.at[3]),
    ]
    blocks = block_out.shape[0] // 4
    through = []
    for part in range(4):
        for i, (src, dst) in enumerate(
            ((block_out, block_out_ref), (residual_grad, residual_grad_ref))
        ):
            rows = pl.ds(part * blocks, blocks)
            sem = 4 + 4 * part + 2 * i
            through.append(
                (
                    pltpu.make_async_copy(src.at[rows], staged.at[i, rows], sems.at[sem]),
                    pltpu.make_async_copy(staged.at[i, rows], dst.at[rows], sems.at[sem + 1]),
                )
            )
    for copy in copies:
        copy.start()
    for into, _ in through:
        into.start()
    gains_grad_ref[...] = gains_grad[...]
    gain_moment_ref[...] = moment_new[...]
    gains_next_ref[...] = gains_new[...]
    rms_ref[...] = rms_new[0:1, 0:1]
    expand_grad_ref[...] = expand_own[...]
    shrink_grad_ref[...] = shrink_own[...]
    for part in range(3):
        columns = slice(part * local, (part + 1) * local)
        heads_grad_ref[part] = heads_own[:, columns]
        heads_cols_ref[part : part + 1, :] = lane_new[0:1, columns]
    merge_rows_ref[...] = lane_new[1, :local]
    expand_cols_ref[...] = lane_new[2, :]
    shrink_rows_ref[...] = lane_new[3, :]
    square[:share, :128] = side_new[...]
    sides = square[:, :128].T
    heads_rows_ref[...] = sides[0, :share]
    merge_cols_ref[...] = sides[1, :share]
    expand_rows_ref[...] = sides[2, :share]
    shrink_cols_ref[...] = sides[3, :share]

    def step(i, own):
        columns = slice(0, own.shape[1])
        return own[...] * side_scale[:, i : i + 1] * lane_scale[i : i + 1, columns]

    square[:share, :local] = merge_own[...]
    merge_grad_ref[...] = square[...].T[:local, :share]
    square[:share, :local] = step(1, merge_own)
    for copy in copies:
        copy.wait()
    expand_next_ref[...] = rows_master[...] - step(2, expand_own)

    def turn(i, carry):
        rows = pl.ds(pl.multiple_of(i * 128, 128), 128)
        rolled = pltpu.roll(window[rows, :], 256 - offset, 1)
        window[rows, :] = rolled
        master[i] = rolled[:, :128].T
        return carry

    blocks_turned = window.shape[0] // 128
    lax.fori_loop(0, blocks_turned // 2, turn, 0)
    for into, out in through[:4]:
        into.wait()
        out.start()
    lax.fori_loop(blocks_turned // 2, blocks_turned, turn, 0)
    for into, out in through[4:]:
        into.wait()
        out.start()
    merge_next_ref[...] = window[merge_at:, :share] - square[...].T[:local, :share]

    shrink_step = step(3, shrink_own)
    for i in range(wide // 128):
        columns = slice(i * 128, (i + 1) * 128)
        shrink_next_ref[:, columns] = master[i, :share, :] - shrink_step[:, columns]
    heads_step = step(0, heads_own)
    heads_master = jnp.concatenate(
        [master[heads_at // 128 + i, :share, :] for i in range((3 * local + 127) // 128)], 1
    )
    for part in range(3):
        columns = slice(part * local, (part + 1) * local)
        heads_next_ref[part] = heads_master[:, columns] - heads_step[:, columns]
    for _, out in through:
        out.wait()


def run_apply(in_hbm, in_vmem, batch_count):
    block_out = in_hbm[0]
    heads_own, merge_own, expand_own, shrink_own = in_vmem[:4]
    width = in_vmem[8].shape[1]
    share, local, wide = merge_own.shape[0], merge_own.shape[1], shrink_own.shape[1]
    side, parts, pair = ((share,), f32), ((3, share, local), f32), ((2, width), f32)
    across, rows = ((local, share), f32), ((share, wide), f32)
    outs = [
        (block_out.shape, f32),
        (block_out.shape, f32),
        parts,
        side,
        ((3, local), f32),
        parts,
        across,
        ((local,), f32),
        side,
        across,
        rows,
        side,
        ((wide,), f32),
        rows,
        rows,
        ((wide,), f32),
        side,
        rows,
        pair,
        pair,
        pair,
        ((1, 1), f32),
    ]
    vm, hbm = pl.BlockSpec(memory_space=pltpu.VMEM), pl.BlockSpec(memory_space=pl.ANY)
    return pl.pallas_call(
        apply_kernel,
        out_shape=tuple(jax.ShapeDtypeStruct(*o) for o in outs),
        in_specs=[hbm] * len(in_hbm) + [vm] * len(in_vmem),
        out_specs=(hbm, hbm) + (vm,) * 20,
        scratch_shapes=[
            pltpu.VMEM((wide + 4 * local, 256), f32),
            pltpu.VMEM(((wide + 4 * local) // 128, 128, 128), f32),
            pltpu.VMEM((share, wide), f32),
            pltpu.VMEM((128, 256), f32),
            pltpu.VMEM((2, *block_out.shape), f32),
            pltpu.SemaphoreType.DMA((20,)),
        ],
        compiler_params=pltpu.CompilerParams(vmem_limit_bytes=VMEM_LIMIT),
        name="apply",
    )(*in_hbm, *in_vmem)


def body(
    residual,
    cotangent,
    lengths,
    gains,
    heads_weight,
    merge_weight,
    expand_weight,
    shrink_weight,
    gain_moment,
    heads_rows,
    heads_cols,
    merge_rows,
    merge_cols,
    expand_rows,
    expand_cols,
    shrink_rows,
    shrink_cols,
):
    seq_len, model_width = residual.shape
    local_width = merge_weight.shape[0]
    batch_count, head_count = lax.axis_size("batch"), lax.axis_size("head")
    heads_cols_w = jnp.transpose(heads_weight, (1, 2, 0)).reshape(3 * local_width, model_width)
    block_out, residual_grad, *shares = run_layer(
        lengths,
        [
            gains,
            gain_moment,
            heads_rows,
            heads_cols,
            merge_rows,
            merge_cols,
            expand_rows,
            expand_cols,
            shrink_rows,
            shrink_cols,
        ],
        residual,
        cotangent,
        (heads_cols_w, merge_weight, expand_weight, shrink_weight),
        batch_count,
        head_count,
    )
    outs = list(
        run_apply(
            [
                block_out,
                residual_grad,
                heads_cols_w,
                merge_weight,
                expand_weight.reshape(batch_count, model_width // batch_count, -1),
                shrink_weight,
            ],
            shares,
            batch_count,
        )
    )
    for i in (0, 1):
        outs[i] = outs[i].reshape(seq_len, model_width)
    for i in (2, 5):
        outs[i] = jnp.transpose(outs[i], (1, 0, 2))
    for i in (14, 17):
        outs[i] = outs[i].T
    outs[21] = outs[21].reshape(())
    return tuple(outs)


def solution(mesh):
    return jax.shard_map(
        body,
        mesh=mesh,
        in_specs=(
            P("batch", None),
            P("batch", None),
            P("batch"),
            P(),
            P(None, None, "head"),
            P("head", None),
            P(None, "head"),
            P("head", None),
            P(),
            P("batch"),
            P(None, "head"),
            P("head"),
            P("batch"),
            P("batch"),
            P("head"),
            P("head"),
            P("batch"),
        ),
        out_specs=(
            P("batch", None),
            P("batch", None),
            P("batch", None, "head"),
            P("batch"),
            P(None, "head"),
            P("batch", None, "head"),
            P("head", "batch"),
            P("head"),
            P("batch"),
            P("head", "batch"),
            P("batch", "head"),
            P("batch"),
            P("head"),
            P("batch", "head"),
            P("head", "batch"),
            P("head"),
            P("batch"),
            P("head", "batch"),
            P(),
            P(),
            P(),
            P(),
        ),
        check_vma=False,
    )
```

time: 839 us -> 166 us (0.20); the launches traced: 828 us -> 166 us
  waiting for transfers between devices: 463 us -> 0 us
  Pallas kernels: 0 us -> 165 us
  matrix products: 117 us -> 0 us
  blocking collectives: 80.4 us -> 0 us
  other arithmetic: 63.6 us -> 0 us
  local copies, waits for them, and re-layouts: 60.2 us -> 0 us
  between operations: 31.4 us -> 1.32 us
  loops' own time: 10.8 us -> 0 us
    psum x4 -> x0, waiting for transfers between devices: 463 us -> none  [the longest x1 247 us: body(): lax.psum((gradients[0], gradients[1], gradients[2], gradients[3]), 'batch')]
    pallas_call x0 -> x2, Pallas kernels: none -> 165 us  [the longest x1 156 us: run_layer(): pl.pallas_call(layer_kernel, out_shape=tuple((jax.ShapeDtypeStruct(*o) fo...]
    dot_general x24 -> x0, matrix products: 80.9 us -> none  [the longest x4 15.1 us: score_block(): jnp.einsum('qhd,khd->hqk', query_blk, key_rows, preferred_element_type=jn...]
    psum x2 -> x0, blocking collectives: 80.4 us -> none  [the longest x1 40.2 us: body(): lax.psum((spread(jnp.sum(heads_sq, (1, 2)), row_off, model_width, 0), spr...]
    reduce_sum x30 -> x0, other arithmetic: 38.3 us -> none  [the longest x2 8.61 us: forward_block(): row_total = jnp.sum(exponent, -1, keepdims=True)]
    sub x2 -> x0, matrix products: 36.4 us -> none  [backward_block(): tangent * prob_grad - row_dot]
    unnamed x143 -> x0, local copies, waits for them, and re-layouts: 18.2 us -> none
    dynamic_update_slice x12 -> x0, local copies, waits for them, and re-layouts: 17.6 us -> none  [the longest x4 15.7 us: body(): lax.scan(backward_block, (empty, empty), (query_blocks, back_blocks, logs...]
  transfers between devices with their start and end apart: 4 -> 0, of which waited for: 4 -> 0; matrix products, arithmetic and copies ran while one was open for 6% -> 0% of each run, Pallas kernels for 0% -> 0%
where the time goes in v1:
time: 166 us
  Pallas kernels  165 us (99%)
    pallas_call x1, Pallas kernels, run_layer(): pl.pallas_call(layer_kernel, out_shape=tuple((jax.ShapeDtypeStruct(*o) fo...  156 us
    pallas_call x1, Pallas kernels, run_apply(): pl.pallas_call(apply_kernel, out_shape=tuple((jax.ShapeDtypeStruct(*o) fo...  8.11 us

profile of v1, /device:TPU:0, one launch (start us, length us, event | category | flops | bytes accessed | tf_op | source)
XLA Modules:
  0.0 165.9 jit_solution(9828211731814922769)
XLA Ops:
  1.3 156.5 %layer.1 = (f32[16,64,768]{2,1,0:T(8,128)}, f32[16,64,768]{2,1,0:T(8,128)}, f32[96,576]{1,0:T(8,128)}, f32[96,192]{1,0:T(8,128)}, f32[96,768]{1,0:T(8,128)}, /*i...) custom-call(s32[1]{0:T(128)S(6)} %copy.39.length_ref, ...), custom_call_target="tpu_custom_call" | custom-call | tf_op jit(solution)/shard_map/layer/pallas_call | solution.py:1319
  157.8 8.1 %apply.1 = (f32[16,64,768]{2,1,0:T(8,128)}, f32[16,64,768]{2,1,0:T(8,128)}, f32[3,96,192]{2,1,0:T(8,128)}, f32[96]{0:T(128)}, f32[3,192]{1,0:T(4,128)}, /*index=...) custom-call(f32[16,64,768]{2,1,0:T(8,128)} %get-tuple-element.58.blo, ...), custom_call_target="tpu_custom_call" | custom-call | tf_op jit(solution)/shard_map/apply/pallas_call | solution.py:1510

commit v2 on v1

--- a/solution.py
+++ b/solution.py
@@ -98,31 +98,31 @@
 
 
 STEPS = {
-    "project": (1, 0, 4, 5),
-    "score": (1, 2, 4, 6),
-    "weigh": (1, 3, 4, 7),
-    "mix": (1, 3, 4, 7),
-    "attn_forward": (8, 6, 7, 9),
-    "feed": (10, 8, 9, 11),
-    "mid_core": (13, 9, 11, 12),
-    "mid_chip": (16, 11, 13, 15),
-    "back_first": (20, 19, 17, 15),
-    "back_second": (20, 19, 17, 16),
-    "back_third": (21, 19, 18, 16),
-    "in_core": (22, 21, 20, 18),
-    "in_chip": (23, 22, 21, 20),
-    "out_core": (15, 20, 23, 13),
-    "out_chip": (21, 22, 25, 23),
-    "merge": (2, 5, 8),
+    "project": (0, 1, 3, 2),
+    "score": (0, 6, 3, 4),
+    "weigh": (1, 6, 3, 4),
+    "mix": (1, 6, 3, 5),
+    "attn_forward": (3, 8, 6, 7),
+    "feed": (7, 10, 9, 8),
+    "mid_core": (8, 11, 10, 9),
+    "mid_chip": (11, 14, 12, 10),
+    "back_first": (16, 15, 13, 11),
+    "back_second": (16, 15, 14, 12),
+    "back_third": (17, 15, 14, 12),
+    "in_core": (18, 17, 15, 13),
+    "in_chip": (19, 18, 17, 16),
+    "out_core": (17, 14, 10, 18),
+    "out_chip": (19, 17, 16, 21),
+    "merge": (2, 4, 6),
     "cast": (0, 1),
     "clear": 5,
-    "wide": (11, 15, 13, 14, 12, 14, 13),
-    "pair": (12, 20, 15, 17, 14, 18, 16, 21, 22, 21, 22, 23, 23),
-    "rest": (22, 23, 23, 20, 22, 20, 24, 22, 24, 23, 24, 24, 24),
-    "update": (24, 25, 25, 25),
-    "last_forward": 11,
-    "first_backward": 9,
-    "all": 26,
+    "wide": (11, 14, 10, 13, 10, 13, 11),
+    "pair": (12, 16, 10, 14, 11, 15, 13, 17, 17, 18, 18, 19, 19),
+    "rest": (15, 20, 16, 19, 19, 17, 18, 18, 18, 20, 20, 20, 20),
+    "update": (20, 20, 21, 21),
+    "last_forward": 10,
+    "first_backward": 8,
+    "all": 22,
 }
 
 

time: 166 us -> 167 us (level)
  no operation moved by 1% of the time
where the time goes in v2:
time: 167 us
  Pallas kernels  165 us (99%)
    pallas_call x1, Pallas kernels, run_layer(): pl.pallas_call(layer_kernel, out_shape=tuple((jax.ShapeDtypeStruct(*o) fo...  157 us
    pallas_call x1, Pallas kernels, run_apply(): pl.pallas_call(apply_kernel, out_shape=tuple((jax.ShapeDtypeStruct(*o) fo...  8.11 us

profile of v2, /device:TPU:0, one launch (start us, length us, event | category | flops | bytes accessed | tf_op | source)
XLA Modules:
  0.0 166.6 jit_solution(3385965288829646651)
XLA Ops:
  1.3 157.2 %layer.1 = (f32[16,64,768]{2,1,0:T(8,128)}, f32[16,64,768]{2,1,0:T(8,128)}, f32[96,576]{1,0:T(8,128)}, f32[96,192]{1,0:T(8,128)}, f32[96,768]{1,0:T(8,128)}, /*i...) custom-call(s32[1]{0:T(128)S(6)} %copy.39.length_ref, ...), custom_call_target="tpu_custom_call" | custom-call | tf_op jit(solution)/shard_map/layer/pallas_call | solution.py:1319
  158.5 8.1 %apply.1 = (f32[16,64,768]{2,1,0:T(8,128)}, f32[16,64,768]{2,1,0:T(8,128)}, f32[3,96,192]{2,1,0:T(8,128)}, f32[96]{0:T(128)}, f32[3,192]{1,0:T(4,128)}, /*index=...) custom-call(f32[16,64,768]{2,1,0:T(8,128)} %get-tuple-element.58.blo, ...), custom_call_target="tpu_custom_call" | custom-call | tf_op jit(solution)/shard_map/apply/pallas_call | solution.py:1510
